TPU v7x, 32 devices: a whole 2x2x4 slice. The times are simulated.
32 devices in a mesh: seq: 8 (over z, y), head: 4 (over x, core).
Axes of the slice: x: 2, y: 2, z: 4, core: 2. Of those that a mesh axis runs over, the one named last changes fastest.
Arguments:
- block_in: bfloat16 [4, 2048, 768], P(None, 'seq'), may hold values from -6 to 6
- cotangent: bfloat16 [4, 2048, 768], P(None, 'seq'), may hold values from -6 to 6
- lengths: int32 [4], replicated, may hold values from 512 to 2048, as said below
- norm_gain: float32 [768], replicated, may hold values from 0.5 to 1.5
- in_proj: float32 [768, 4, 838], P(None, 'head'), may hold values from -0.21875 to 0.21875
- conv_params: float32 [5, 4, 448], P(None, 'head'), may hold values from -2 to 2
- head_params: float32 [3, 24], P(None, 'head'), as said below
- gate_gain: float32 [1536], P('head'), may hold values from 0.5 to 1.5
- out_proj: float32 [1536, 768], P('head'), may hold values from -0.15625 to 0.15625
- norm_gain_momentum: float32 [768], replicated, may hold values from -224 to 224
- in_proj_momentum: float32 [768, 4, 838], P(None, 'head'), may hold values from -112 to 112
- conv_momentum: float32 [5, 4, 448], P(None, 'head'), may hold values from -112 to 112
- head_momentum: float32 [3, 24], P(None, 'head'), may hold values from -512 to 512
- gate_gain_momentum: float32 [1536], P('head'), may hold values from -256 to 256
- out_proj_momentum: float32 [1536, 768], P('head'), may hold values from -384 to 384
- norm_gain_average: float32 [768], replicated, may hold values from 0.5 to 1.5
- in_proj_average: float32 [768, 4, 838], P(None, 'head'), may hold values from -0.21875 to 0.21875
- conv_average: float32 [5, 4, 448], P(None, 'head'), may hold values from -2 to 2
- head_average: float32 [3, 24], P(None, 'head'), may hold values from -1 to 1
- gate_gain_average: float32 [1536], P('head'), may hold values from 0.5 to 1.5
- out_proj_average: float32 [1536, 768], P('head'), may hold values from -0.15625 to 0.15625
Outputs:
- block_out: bfloat16 [4, 2048, 768], P(None, 'seq')
- input_grad: float32 [4, 2048, 768], P(None, 'seq')
- norm_gain_new: float32 [768], replicated
- norm_gain_moment: float32 [768], replicated
- norm_gain_mean: float32 [768], replicated
- in_proj_new: float32 [768, 4, 838], P(None, 'head')
- in_proj_moment: float32 [768, 4, 838], P(None, 'head')
- in_proj_mean: float32 [768, 4, 838], P(None, 'head')
- conv_new: float32 [5, 4, 448], P(None, 'head')
- conv_moment: float32 [5, 4, 448], P(None, 'head')
- conv_mean: float32 [5, 4, 448], P(None, 'head')
- head_new: float32 [3, 24], P(None, 'head')
- head_moment: float32 [3, 24], P(None, 'head')
- head_mean: float32 [3, 24], P(None, 'head')
- gate_gain_new: float32 [1536], P('head')
- gate_gain_moment: float32 [1536], P('head')
- gate_gain_mean: float32 [1536], P('head')
- out_proj_new: float32 [1536, 768], P('head')
- out_proj_moment: float32 [1536, 768], P('head')
- out_proj_mean: float32 [1536, 768], P('head')
Inputs may be any that keep to these rules, and one draw needn't show every extreme that they name: `lengths`: in every draw one sequence has all 2048 slots real. `head_params`: row 0 lies in -5.1 to -4.1, row 1 (log decay rate) in log(0.3 / (2048 * 0.0165)) to log(2), and row 2 in 0.4 to 2.4.
All inputs are finite; a program needn't handle non-finite values.
Results may differ from a plain program's by a relative error of at most 0.01.
The roundings to bfloat16 on the way count: a program that leaves them out, or rounds other values in their place, can miss the bound.
Values may be sent and summed in bfloat16 or wider, within the bound.
No kernel may reach another device: no remote copies, remote signals or barrier semaphores. Data moves between devices by JAX's collectives and lax.ppermute only.
A program may use at most 192 MiB of HBM per device.

v0:
```python
import math

import jax
import jax.numpy as jnp
from jax import lax
from jax.sharding import PartitionSpec as P

HDIM = 64
CONV = 4
INNER = 1536


EPSILON = 1e-05
MOMENTUM = 0.5
AVERAGE = 0.5
RATES = (0.15, 0.1, 0.5, 0.05, 0.15, 0.02)
HIGHEST = lax.Precision.HIGHEST


def passed_along(array, axis, by):
    length = lax.axis_size(axis)
    pairs = [(i, i + by) for i in range(length) if 0 <= i + by < length]
    return lax.ppermute(array, axis, pairs)


def prefix_2(array, axis, combine, identity):
    length, here = (lax.axis_size(axis), lax.axis_index(axis))
    everything = jax.tree.map(
        lambda part, kind: lax.all_gather(part.astype(kind), axis),
        array,
        (jnp.bfloat16, jnp.bfloat16),
    )
    start = jax.tree.map(
        lambda part, zero: jnp.broadcast_to(jnp.asarray(zero, part.dtype), part.shape),
        array,
        identity,
    )

    def hop(k, before):
        reached = k < here
        new = combine(
            before, jax.tree.map(lambda part, own: part[k].astype(own.dtype), everything, array)
        )
        return jax.tree.map(lambda a, b: jnp.where(reached, a, b), new, before)

    return lax.fori_loop(0, length, hop, start)


def entering(array, axis, join, neutral):
    count = lax.axis_size(axis)
    place = lax.axis_index(axis)
    ahead = count - 1 - place
    gathered = jax.tree.map(
        lambda a, kind: lax.all_gather(a.astype(kind), axis),
        array,
        jax.tree.map(lambda a: jnp.bfloat16 if a.dtype == jnp.float32 else a.dtype, array),
    )
    state = jax.tree.map(lambda a, e: jnp.zeros_like(a) + jnp.asarray(e, a.dtype), array, neutral)

    def one(hop, state):
        source = count - 1 - hop
        return join(
            state,
            jax.tree.map(
                lambda a, own: lax.dynamic_index_in_dim(a, source, 0, False).astype(own.dtype),
                gathered,
                array,
            ),
        )

    return lax.fori_loop(0, ahead, one, state)


def span_parts(x_values, b_rows, c_rows, decays, step_sizes):
    running = jnp.cumsum(decays, axis=0)
    length = running.shape[0]
    places = jnp.arange(length)
    causal = (places[:, None] >= places[None, :])[:, :, None]
    scores = jnp.dot(c_rows, b_rows.T, precision=HIGHEST)
    exponents = jnp.where(causal, running[:, None, :] - running[None, :, :], 0.0)
    weights = jnp.where(causal, jnp.exp(exponents), 0.0) * scores[:, :, None]
    inside = jnp.einsum(
        "tsh,shp->thp", weights, step_sizes[:, :, None] * x_values, precision=HIGHEST
    )
    ending = running[-1]
    tail_weights = jnp.exp(ending[None, :] - running) * step_sizes
    fresh_state = jnp.einsum(
        "shp,sn->hpn", tail_weights[:, :, None] * x_values, b_rows, precision=HIGHEST
    )
    return (inside, fresh_state, jnp.exp(ending), running)


def carried_term(c_rows, state_in, running):
    return (
        jnp.einsum("tn,hpn->thp", c_rows, state_in, precision=HIGHEST)
        * jnp.exp(running)[:, :, None]
    )


def state_pull(c_rows, d_values, running):
    return jnp.einsum(
        "thp,tn->hpn", d_values * jnp.exp(running)[:, :, None], c_rows, precision=HIGHEST
    )


def mixer_parts(x_values, both_rows, raw_steps, head_params):
    step_sizes = jax.nn.softplus(raw_steps + head_params[0])
    decays = -jnp.exp(head_params[1]) * step_sizes
    inside, fresh_state, totals, running = jax.vmap(span_parts)(
        x_values, both_rows[:, :, 0], both_rows[:, :, 1], decays, step_sizes
    )
    return (inside + head_params[2][:, None] * x_values, fresh_state, totals, running)


def mixer_full(x_values, both_rows, raw_steps, head_params, state_in):
    local_out, fresh_state, totals, running = mixer_parts(
        x_values, both_rows, raw_steps, head_params
    )
    return (
        local_out + jax.vmap(carried_term)(both_rows[:, :, 1], state_in, running),
        fresh_state,
        totals,
    )


def convolve(padded, taps):
    length = padded.shape[1] - (CONV - 1)
    summed = taps[CONV]
    for offset in range(CONV):
        summed = summed + taps[offset] * padded[:, offset : offset + length]
    return jax.nn.silu(summed)


def chain_forward(earlier, later):
    return (earlier[0] * later[0], later[0][..., None, None] * earlier[1] + later[1])


def chain_backward(earlier, later):
    return (later[0] * earlier[0], later[1] + later[0][..., None, None] * earlier[1])


def advance(weight, gradient, moment, average, rate):
    moment_new = MOMENTUM * moment + gradient
    weight_new = weight - rate * (gradient + MOMENTUM * moment_new)
    average_new = AVERAGE * average + (1.0 - AVERAGE) * weight_new
    return (weight_new, moment_new, average_new)


def shards(
    block_in,
    cotangent,
    lengths,
    norm_gain,
    in_proj,
    conv_params,
    head_params,
    gate_gain,
    out_proj,
    norm_gain_momentum,
    in_proj_momentum,
    conv_momentum,
    head_momentum,
    gate_gain_momentum,
    out_proj_momentum,
    norm_gain_average,
    in_proj_average,
    conv_average,
    head_average,
    gate_gain_average,
    out_proj_average,
):
    seq_count, blk_rows, width = block_in.shape
    row_count = seq_count * blk_rows
    head_count = head_params.shape[1]
    z_width = head_count * HDIM
    c_width = conv_params.shape[2]
    s_width = (c_width - z_width) // 2
    block_f = block_in.astype(jnp.float32)
    scale = lax.rsqrt(jnp.mean(block_f * block_f, axis=-1, keepdims=True) + EPSILON)
    unit_in = block_f * scale
    normed = (unit_in * norm_gain).astype(jnp.bfloat16).reshape(row_count, width)
    in_low = in_proj.reshape(width, -1).astype(jnp.bfloat16)
    projected = jnp.dot(normed, in_low, preferred_element_type=jnp.float32).reshape(
        seq_count, blk_rows, -1
    )
    gate_pre = projected[..., :z_width]
    mixed = projected[..., z_width : z_width + c_width]
    raw_steps = projected[..., z_width + c_width :]
    edge_rows = passed_along(mixed[:, blk_rows - (CONV - 1) :, :], "seq", 1)
    padded = jnp.concatenate([edge_rows, mixed], axis=1)
    taps = conv_params[:, 0, :]
    active = convolve(padded, taps)
    x_values = active[..., :z_width].reshape(seq_count, blk_rows, head_count, HDIM)
    own_rows = active[..., z_width:].reshape(seq_count, blk_rows, 2, s_width).astype(jnp.bfloat16)
    both_rows = lax.all_gather(own_rows, "head", axis=3, tiled=True).astype(jnp.float32)
    local_out, fresh_state, totals, running = mixer_parts(
        x_values, both_rows, raw_steps, head_params
    )
    prefix = prefix_2(
        (totals, fresh_state),
        "seq",
        chain_forward,
        (jnp.ones_like(totals), jnp.zeros_like(fresh_state)),
    )
    state_in = prefix[1]
    mixer_out = local_out + jax.vmap(carried_term)(both_rows[:, :, 1], state_in, running)
    mixer_flat = mixer_out.reshape(seq_count, blk_rows, z_width)
    gate_act = jax.nn.silu(gate_pre)
    gated = mixer_flat * gate_act
    squares = lax.psum(jnp.sum(gated * gated, axis=-1), "head")
    rstd = lax.rsqrt(squares / INNER + EPSILON)[..., None]
    unit_out = gated * rstd
    out_in = (unit_out * gate_gain).astype(jnp.bfloat16).reshape(row_count, z_width)
    out_low = out_proj.astype(jnp.bfloat16)
    partial_out = jnp.dot(out_in, out_low, preferred_element_type=jnp.float32)
    branch = lax.psum(partial_out, "head").reshape(seq_count, blk_rows, width)
    places = lax.axis_index("seq") * blk_rows + jnp.arange(blk_rows, dtype=jnp.int32)
    live_mask = (places[None, :] < lengths[:, None]).astype(jnp.float32)[..., None]
    block_out = (live_mask * (block_f + branch)).astype(jnp.bfloat16)
    incoming = live_mask * cotangent.astype(jnp.float32)
    incoming_low = incoming.astype(jnp.bfloat16).reshape(row_count, width)
    g_out = lax.dot_general(
        out_in, incoming_low, (((0,), (0,)), ((), ())), preferred_element_type=jnp.float32
    )
    d_out_in = lax.dot_general(
        incoming_low, out_low, (((1,), (1,)), ((), ())), preferred_element_type=jnp.float32
    ).reshape(seq_count, blk_rows, z_width)
    g_ggain = jnp.sum(d_out_in * unit_out, axis=(0, 1))
    d_unit = d_out_in * gate_gain
    across = lax.psum(jnp.sum(d_unit * unit_out, axis=-1), "head")
    d_gated = rstd * (d_unit - unit_out * (across / INNER)[..., None])
    sigma = jax.nn.sigmoid(gate_pre)
    d_mixer = (d_gated * gate_act).reshape(seq_count, blk_rows, head_count, HDIM)
    d_gate = d_gated * mixer_flat * sigma * (1.0 + gate_pre * (1.0 - sigma))
    pulled = jax.vmap(state_pull)(both_rows[:, :, 1], d_mixer, running)
    suffix = entering(
        (totals, pulled), "seq", chain_backward, (jnp.ones_like(totals), jnp.zeros_like(pulled))
    )
    after = suffix[1]
    d_totals = jnp.sum(after * state_in, axis=(2, 3))
    unused_out, mixer_pull = jax.vjp(
        mixer_full, x_values, both_rows, raw_steps, head_params, state_in
    )
    d_values, d_both, d_raw, g_heads, unused_state = mixer_pull((d_mixer, after, d_totals))
    d_own = lax.psum_scatter(
        d_both.astype(jnp.bfloat16), "head", scatter_dimension=3, tiled=True
    ).astype(jnp.float32)
    d_active = jnp.concatenate(
        [
            d_values.reshape(seq_count, blk_rows, z_width),
            d_own.reshape(seq_count, blk_rows, 2 * s_width),
        ],
        axis=-1,
    )
    unused_conv, conv_pull = jax.vjp(convolve, padded, taps)
    d_padded, g_taps = conv_pull(d_active)
    spill = passed_along(d_padded[:, : CONV - 1, :], "seq", -1)
    d_mixed = d_padded[:, CONV - 1 :, :] + jnp.pad(
        spill, ((0, 0), (blk_rows - (CONV - 1), 0), (0, 0))
    )
    d_proj = (
        jnp.concatenate([d_gate, d_mixed, d_raw], axis=-1)
        .astype(jnp.bfloat16)
        .reshape(row_count, -1)
    )
    g_in = lax.dot_general(
        normed, d_proj, (((0,), (0,)), ((), ())), preferred_element_type=jnp.float32
    ).reshape(width, 1, -1)
    partial_back = lax.dot_general(
        d_proj, in_low, (((1,), (1,)), ((), ())), preferred_element_type=jnp.float32
    )
    d_normed = lax.psum(partial_back, "head").reshape(seq_count, blk_rows, width)
    g_ngain = jnp.sum(d_normed * unit_in, axis=(0, 1))
    d_unit_in = d_normed * norm_gain
    input_grad = (
        scale * (d_unit_in - unit_in * jnp.mean(d_unit_in * unit_in, axis=-1, keepdims=True))
        + incoming
    )
    seq_devices = lax.axis_size("seq")
    root = math.sqrt(seq_count * blk_rows * seq_devices)
    g_ngain, g_in, g_taps, g_heads, g_ggain, g_out = lax.psum(
        (g_ngain, g_in, g_taps, g_heads, g_ggain, g_out), "seq"
    )
    in_triple = advance(in_proj, g_in, in_proj_momentum, in_proj_average, RATES[1] / root)
    out_triple = advance(out_proj, g_out, out_proj_momentum, out_proj_average, RATES[5] / root)
    ng_triple = advance(norm_gain, g_ngain, norm_gain_momentum, norm_gain_average, RATES[0] / root)
    conv_triple = advance(
        conv_params, g_taps.reshape(conv_params.shape), conv_momentum, conv_average, RATES[2] / root
    )
    head_triple = advance(head_params, g_heads, head_momentum, head_average, RATES[3] / root)
    gg_triple = advance(gate_gain, g_ggain, gate_gain_momentum, gate_gain_average, RATES[4] / root)
    return (
        block_out,
        input_grad,
        ng_triple[0],
        ng_triple[1],
        ng_triple[2],
        in_triple[0],
        in_triple[1],
        in_triple[2],
        conv_triple[0],
        conv_triple[1],
        conv_triple[2],
        head_triple[0],
        head_triple[1],
        head_triple[2],
        gg_triple[0],
        gg_triple[1],
        gg_triple[2],
        out_triple[0],
        out_triple[1],
        out_triple[2],
    )


def solution(mesh):
    placed = (
        P(None, "seq", None),
        P(None, "seq", None),
        P(),
        P(),
        P(None, "head", None),
        P(None, "head", None),
        P(None, "head"),
        P("head"),
        P("head", None),
        P(),
        P(None, "head", None),
        P(None, "head", None),
        P(None, "head"),
        P("head"),
        P("head", None),
        P(),
        P(None, "head", None),
        P(None, "head", None),
        P(None, "head"),
        P("head"),
        P("head", None),
    )
    return jax.shard_map(
        shards,
        mesh=mesh,
        in_specs=placed,
        out_specs=(
            P(None, "seq", None),
            P(None, "seq", None),
            P(),
            P(),
            P(),
            P(None, "head", None),
            P(None, "head", None),
            P(None, "head", None),
            P(None, "head", None),
            P(None, "head", None),
            P(None, "head", None),
            P(None, "head"),
            P(None, "head"),
            P(None, "head"),
            P("head"),
            P("head"),
            P("head"),
            P("head", None),
            P("head", None),
            P("head", None),
        ),
        check_vma=False,
    )
```

profile of v0, /device:TPU:0, one launch (start us, length us, event | category | flops | bytes accessed | tf_op | source)
XLA Modules:
  0.0 609.3 jit_solution(8184827484847975216)
XLA Ops:
  16.7 4.9 collective-permute-start
  24.8 7.2 %reduce-window.14 = f32[4,6,2,128]{3,2,1,0:T(2,128)S(1)} reduce-window(f32[4,6,2,128]{3,2,1,0:T(2,128)S(1)} %copy.221, f32[]{:T(128)} %constant.112.clone.1), window={size=1x1x1x128 pad=0_0x0_0x0_0x127_0}, to_apply=%region_1.2 | reduce-window | flops 780288 | bytes 49156 | tf_op jit(solution)/shard_map/reduce-window
  37.7 4.8 fusion.44
  43.7 7.2 %all_gather.21 = bf16[4,256,2,128]{1,0,2,3:T(4,128)(2,1)S(1)} all-gather(bf16[4,256,2,32]{1,0,2,3:T(4,128)(2,1)S(1)} %copy.228), channel_id=1, replica_groups=mesh['seq'=8,'head'=4] {'head'}, dimensions={3}, use_global_device_ids=true | all-gather | bytes 655360 | tf_op jit(solution)/shard_map/all_gather | solution.py:195
  53.8 26.7 %all-gather = bf16[32,1,6]{2,1,0:T(2,128)(2,1)S(1)} all-gather(bf16[4,1,6]{2,1,0:T(2,128)(2,1)S(1)} %copy.231), channel_id=2, replica_groups=mesh['seq'=8,'head'=4] {'seq'}, dimensions={0}, use_global_device_ids=true | all-gather | bytes 432 | tf_op jit(solution)/shard_map/all_gather | solution.py:29
  85.4 28.0 %all-gather.6.cloned.1.call-done = bf16[32,6,64,128]{3,2,1,0:T(8,128)(2,1)} async-done(((bf16[4,6,64,128]{3,2,1,0:T(8,128)(2,1)}), bf16[32,6,64,128]{3,2,1,0:T(8,128)(2,1)}) %all-gather.6.cloned.1.call-update) | async-done | bytes 3145744 | tf_op jit(solution)/shard_map/all_gather | solution.py:29
  113.4 9.7 %while.29 = (s32[]{:T(128)}, f32[4,6,64,128]{3,2,1,0:T(8,128)S(1)}, s32[]{:T(128)}, bf16[8,4,6]{2,1,0:T(4,128)(2,1)S(1)}, bf16[8,4,6,64,128]{4,3,2,1,0:T(8,128)(2,1)}, /*index=5*/s32[]{:T(128)}, s32[]{:T(128)}) while((s32[]{:T(128)}, f32[4,6,64,128]{3,2,1,0:T(8,128)S(1)}, s32[]{:T(128)}, bf16[8,4,6]{2,1,0:T(4,128)(2,1)S(1)}, ...), condition=%wide.region_4.5_spmd.clone, body=%wide.region_3.4_spmd.clone.sunk | while | flops 983068 | bytes 1966425 | solution.py:46
  124.4 7.2 %fusion.61 = f32[4,256,6,64]{1,3,2,0:T(8,128)S(1)} fusion(f32[4,256,6,64]{1,3,2,0:T(8,128)S(1)} %fusion.117, f32[4,256,6,64]{1,3,2,0:T(8,128)S(1)} %bitcast.206, f32[4,256,256]{2,1,0:T(8,128)S(1)} %copy-done.36, f32[4,256,6]{1,2,0:T(8,128)S(1)} %copy-done.41, pred[256,256]{1,0:T(8,128)(4,1)S(1)} %iota_compare_fusion, f32[4,256,6]{1,2,0:T(8,128)S(1)} %copy.235, ...), kind=kOutput, calls=%fused_computation.94 | convolution fusion | flops 1216217088 | bytes 5906456 | tf_op jit(solution)/shard_map/vmap(tsh,shp->thp)/dot_general | solution.py:82
  134.1 5.7 psum.70
  139.9 4.4 multiply_reduce_fusion.4
  144.3 6.5 %psum.72 = f32[4,256]{1,0:T(4,128)S(1)} all-reduce(f32[4,256]{1,0:T(4,128)S(1)} %get-tuple-element.397), channel_id=1, replica_groups=mesh['seq'=8,'head'=4] {'head'}, use_global_device_ids=true, to_apply=%region_9.10 | all-reduce | flops 1024 | bytes 8192 | tf_op jit(solution)/shard_map/psum | solution.py:230
  150.8 6.2 %multiply_reduce_fusion.5 = (f32[384]{0:T(512)}, f32[4,256,384]{1,2,0:T(8,128)S(1)}, bf16[4,256,384]{1,2,0:T(8,128)(2,1)}, bf16[4,256,384]{1,2,0:T(8,128)(2,1)}) fusion(f32[4,256,448]{1,2,0:T(8,128)} %copy-done.6, f32[4,256,838]{1,2,0:T(8,128)} %copy-done, f32[4,256]{1,0:T(4,128)S(1)} %broadcast_multiply_fusion.5, f32[4,256,384]{1,2,0:T(8,128)} %copy-done.18, ...), kind=kLoop, calls=%fused_computation.96 | loop fusion | flops 8257152 | bytes 11021312 | tf_op jit(solution)/shard_map/transpose(jvp())/reduce_sum | solution.py:112
  163.2 11.7 %fusion.16 = (f32[4,256,6]{1,2,0:T(8,128)}, f32[4,256,6]{1,2,0:T(8,128)}, f32[4,256,256]{2,1,0:T(8,128)}) fusion(f32[4,256,256]{2,1,0:T(8,128)} %fusion.123, f32[4,256,6]{1,2,0:T(8,128)} %copy.226, pred[256,256]{1,0:T(8,128)(4,1)S(1)} %iota_compare_fusion, f32[4,6,64,256]{3,2,1,0:T(8,128)S(1)} %bitcast.201, f32[4,256,6,64]{1,3,2,0:T(8,128)} %bitcast.207, ...), kind=kOutput, calls=%fused_computation.24 | convolution fusion | flops 1225379840 | bytes 5406720 | tf_op jit(solution)/shard_map/transpose(jvp(vmap(tsh,shp->thp)))/dot_general | solution.py:82
  192.0 25.6 %all-gather.8.cloned.1.call-done = bf16[32,6,64,128]{3,2,1,0:T(8,128)(2,1)} async-done(((bf16[4,6,64,128]{3,2,1,0:T(8,128)(2,1)}), bf16[32,6,64,128]{3,2,1,0:T(8,128)(2,1)}) %all-gather.8.cloned.1.call-update) | async-done | bytes 3145744 | tf_op jit(solution)/shard_map/all_gather | solution.py:54
  217.7 9.0 %while.28 = (s32[]{:T(128)}, f32[4,6,64,128]{3,2,1,0:T(8,128)S(1)}, s32[]{:T(128)}, bf16[8,4,6,64,128]{4,3,2,1,0:T(8,128)(2,1)}, bf16[8,4,6]{2,1,0:T(4,128)(2,1)...) while((s32[]{:T(128)}, f32[4,6,64,128]{3,2,1,0:T(8,128)S(1)}, s32[]{:T(128)}, ...), condition=%wide.region_11.12_spmd, body=%wide.region_10.11_spmd.sunk | while | flops 589854 | bytes 1966467 | solution.py:71
  236.0 8.8 %fusion.57 = (f32[4,256,6]{1,2,0:T(8,128)}, f32[4,256,6]{1,2,0:T(8,128)S(1)}, f32[4,256,6,64]{1,3,2,0:T(8,128)}) fusion(f32[4,256,6,64]{1,3,2,0:T(8,128)} %bitcast.209, f32[4,256,6,64]{1,3,2,0:T(8,128)} %fusion.119, f32[4,256,6]{1,2,0:T(8,128)S(1)} %copy-done.44, f32[4,256,6]{1,2,0:T(8,128)S(1)} %copy.233, f32[4,256,6,64]{1,3,2,0:T(8,128)S(1)} %bitcast.203, ...), kind=kOutput, calls=%fused_computation.87 | convolution fusion | flops 1217777664 | bytes 9101336 | tf_op jit(solution)/shard_map/transpose(jvp(vmap(tsh,shp->thp)))/dot_general | solution.py:82
  250.4 30.2 %reduce-window.16 = f32[4,6,2,128]{3,2,1,0:T(2,128)S(1)} reduce-window(f32[4,6,2,128]{3,2,1,0:T(2,128)S(1)} %copy.253, f32[]{:T(128)} %constant.112.clone.1), window={size=1x1x1x128 pad=0_0x0_0x0_0x0_127}, to_apply=%region_21.22 | reduce-window | flops 780288 | bytes 49156 | tf_op jit(solution)/shard_map/reduce-window.2
  287.4 6.0 multiply_reduce_fusion.3
  298.9 6.3 %pad_add_fusion = f32[4,259,448]{1,2,0:T(8,128)} fusion(f32[4,256,448]{1,2,0:T(8,128)} %copy-done.3, f32[4,256,448]{1,2,0:T(8,128)} %copy-done.4, f32[4,256,448]{1,2,0:T(8,128)} %copy-done.5, f32[4,256,448]{1,2,0:T(8,128)S(1)} %get-tuple-element.464), kind=kLoop, calls=%fused_computation.50 | loop fusion | flops 1392384 | bytes 9196544 | tf_op jit(solution)/shard_map/transpose(jvp())/add_any | solution.py:130
  323.0 109.3 %all-reduce.29.cloned.1.call-done = (f32[4,256,768]{2,1,0:T(8,128)}, f32[4,256,768]{2,1,0:T(8,128)}) async-done(((f32[4,256,768]{2,1,0:T(8,128)}, f32[4,256,768]{2,1,0:T(8,128)}), (f32[4,256,768]{2,1,0:T(8,128)}, f32[4,256,768]{2,1,0:T(8,128)})) %all-reduce.29.cloned.1.call-update) | async-done | bytes 6291472 | tf_op jit(solution)/shard_map/psum | solution.py:216
  435.3 39.4 %all-reduce.18 = (f32[768]{0:T(1024)S(1)}, f32[5,1,448]{2,1,0:T(1,128)S(1)}, f32[3,6]{1,0:T(4,128)S(1)}, f32[384]{0:T(512)S(1)}) all-reduce(f32[768]{0:T(1024)S(1)} %get-tuple-element.391, f32[5,1,448]{2,1,0:T(1,128)S(1)} %reshape.307, f32[3,6]{1,0:T(4,128)S(1)} %pad_add_fusion.3, ...), channel_id=1, replica_groups=mesh['seq'=8,'head'=4] {'seq'}, use_global_device_ids=true, to_apply=%region_26.27 | all-reduce | flops 3410 | bytes 27280 | tf_op jit(solution)/shard_map/psum | solution.py:281
  477.2 5.4 fusion.21
  482.6 100.4 %all-reduce.27.cloned.1.call-done = (f32[768,1,838]{0,2,1:T(8,128)}, f32[384,768]{1,0:T(8,128)}) async-done(((f32[768,1,838]{0,2,1:T(8,128)}, f32[384,768]{1,0:T(8,128)}), (f32[768,1,838]{0,2,1:T(8,128)}, f32[384,768]{1,0:T(8,128)})) %all-reduce.27.cloned.1.call-update) | async-done | bytes 3754000 | tf_op jit(solution)/shard_map/psum | solution.py:281
  583.0 4.9 fusion.37
  (331 shorter events, 135.8 us)
Async XLA Ops:
  7.2 106.2 %all-gather.6.cloned.1.call-start = ((), (), s32[]{:S(2)}) async-start(), calls=%async_computation | async-start | bytes 3538944 | tf_op jit(solution)/shard_map/all_gather | solution.py:29
  16.7 19.6 %collective-permute-start = (f32[4,3,448]{2,0,1:T(4,128)S(1)}, f32[4,3,448]{2,0,1:T(4,128)S(1)}, u32[]{:S(2)}, u32[]{:S(2)}) collective-permute-start(f32[4,3,448]{2,0,1:T(4,128)S(1)} %copy.218), channel_id=1, source_target_pairs={{0,4},{4,8},{8,12},{12,16},{16,20},{20,24},{24,28},{1,5},{5,9},{9,... | collective-permute-start | bytes 64520 | tf_op jit(solution)/shard_map/ppermute | solution.py:23
  32.8 20.3 %copy-start.10 = (f32[4,6,2,128]{1,0,3,2:T(4,128)}, f32[4,6,2,128]{1,0,3,2:T(4,128)S(1)}, u32[]{:S(2)}) copy-start(f32[4,6,2,128]{1,0,3,2:T(4,128)S(1)} %copy.280) | copy-start | bytes 73732
  42.6 81.4 %copy-start.7 = (f32[4,256,384]{1,2,0:T(8,128)}, f32[4,256,384]{1,2,0:T(8,128)S(1)}, u32[]{:S(2)}) copy-start(f32[4,256,384]{1,2,0:T(8,128)S(1)} %slice.135) | copy-start | bytes 4718596
  53.0 164.6 %all-gather.8.cloned.1.call-start = ((), (), s32[]{:S(2)}) async-start(), calls=%async_computation.1 | async-start | bytes 3538944 | tf_op jit(solution)/shard_map/all_gather | solution.py:54
  83.1 40.9 %copy-start.43 = (f32[4,256,6]{1,2,0:T(8,128)}, f32[4,256,6]{1,2,0:T(8,128)S(1)}, u32[]{:S(2)}) copy-start(f32[4,256,6]{1,2,0:T(8,128)S(1)} %copy.217) | copy-start | bytes 73732
  83.9 56.0 %copy-start.57 = (f32[4,256]{1,0:T(4,128)}, f32[4,256]{1,0:T(4,128)S(1)}, u32[]{:S(2)}) copy-start(f32[4,256]{1,0:T(4,128)S(1)} %compare_convert_fusion) | copy-start | bytes 12292
  84.2 72.9 %copy-start.14 = (bf16[4,256,1,128]{3,1,0,2:T(8,128)(2,1)}, bf16[4,256,1,128]{3,1,0,2:T(8,128)(2,1)S(1)}, u32[]{:S(2)}) copy-start(bf16[4,256,1,128]{3,1,0,2:T(8,128)(2,1)S(1)} %copy.291) | copy-start | bytes 786436
  158.7 127.6 %all-reduce.25.cloned.1.call-start = ((), (), s32[]{:S(2)}) async-start(), calls=%async_computation.2 | async-start | bytes 1048576
  236.0 196.3 %all-reduce.29.cloned.1.call-start = ((), (), s32[]{:S(2)}) async-start(), calls=%async_computation.4 | async-start | bytes 12582912 | tf_op jit(solution)/shard_map/psum | solution.py:216
  247.9 33.3 %copy-start.75 = (f32[6]{0:T(128)S(1)}, f32[6]{0:T(128)}, u32[]{:S(2)}) copy-start(f32[6]{0:T(128)} %copy-done.74) | copy-start | bytes 76
  249.1 32.6 %copy-start.45 = (f32[4,256,6]{1,2,0:T(8,128)S(1)}, f32[4,256,6]{1,2,0:T(8,128)}, u32[]{:S(2)}) copy-start(f32[4,256,6]{1,2,0:T(8,128)} %get-tuple-element.403) | copy-start | bytes 73732
  297.4 7.8 %collective-permute-start.1 = (f32[4,3,448]{2,0,1:T(4,128)S(1)}, f32[4,3,448]{2,0,1:T(4,128)S(1)}, u32[]{:S(2)}, u32[]{:S(2)}) collective-permute-start(f32[4,3,448]{2,0,1:T(4,128)S(1)} %copy.243), channel_id=1, source_target_pairs={{4,0},{8,4},{12,8},{16,12},{20,16},{24,20},{28,24},{5,1},{9,5},{13... | collective-permute-start | bytes 64520 | tf_op jit(solution)/shard_map/ppermute | solution.py:23
  313.1 269.9 %all-reduce.27.cloned.1.call-start = ((), (), s32[]{:S(2)}) async-start(), calls=%async_computation.3 | async-start | bytes 7520256 | tf_op jit(solution)/shard_map/psum | solution.py:281
  432.3 42.4 %copy-start.64 = (f32[384]{0:T(512)S(1)}, f32[384]{0:T(512)}, u32[]{:S(2)}) copy-start(f32[384]{0:T(512)} %param.32) | copy-start | bytes 4612
  432.3 42.4 %copy-start.78 = (f32[384]{0:T(512)S(1)}, f32[384]{0:T(512)}, u32[]{:S(2)}) copy-start(f32[384]{0:T(512)} %param.44) | copy-start | bytes 4612
  432.3 42.4 %copy-start.79 = (f32[384]{0:T(512)S(1)}, f32[384]{0:T(512)}, u32[]{:S(2)}) copy-start(f32[384]{0:T(512)} %param.38) | copy-start | bytes 4612
  432.3 43.0 %copy-start.80 = (f32[3,6]{1,0:T(4,128)S(1)}, f32[3,6]{1,0:T(4,128)}, u32[]{:S(2)}) copy-start(f32[3,6]{1,0:T(4,128)} %param.43) | copy-start | bytes 220
  432.3 43.0 %copy-start.81 = (f32[3,6]{1,0:T(4,128)S(1)}, f32[3,6]{1,0:T(4,128)}, u32[]{:S(2)}) copy-start(f32[3,6]{1,0:T(4,128)} %param.37) | copy-start | bytes 220
  432.3 43.6 %copy-start.76 = (f32[768]{0:T(1024)S(1)}, f32[768]{0:T(1024)}, u32[]{:S(2)}) copy-start(f32[768]{0:T(1024)} %param.40) | copy-start | bytes 9220
  432.3 43.6 %copy-start.77 = (f32[768]{0:T(1024)S(1)}, f32[768]{0:T(1024)}, u32[]{:S(2)}) copy-start(f32[768]{0:T(1024)} %param.34) | copy-start | bytes 9220
  432.3 44.2 %copy-start.39 = (f32[5,1,448]{2,1,0:T(1,128)S(1)}, f32[5,1,448]{2,1,0:T(1,128)}, u32[]{:S(2)}) copy-start(f32[5,1,448]{2,1,0:T(1,128)} %param.30) | copy-start | bytes 26884
  432.3 44.2 %copy-start.61 = (f32[5,1,448]{2,1,0:T(1,128)S(1)}, f32[5,1,448]{2,1,0:T(1,128)}, u32[]{:S(2)}) copy-start(f32[5,1,448]{2,1,0:T(1,128)} %param.42) | copy-start | bytes 26884
  432.4 44.2 %copy-start.62 = (f32[5,1,448]{2,1,0:T(1,128)S(1)}, f32[5,1,448]{2,1,0:T(1,128)}, u32[]{:S(2)}) copy-start(f32[5,1,448]{2,1,0:T(1,128)} %param.36) | copy-start | bytes 26884
  (71 other events, 284.2 us)
Sparse Core Ops, SparseCore 0:
  53.1 60.2 all-gather.5
  158.8 58.6 all-gather.7
  236.0 30.4 all-reduce.24
  313.2 119.0 all-reduce.28
  436.4 146.4 all-reduce.26
where the time goes:
time: 618 us; the launch traced here: 609 us
  waiting for transfers between devices  263 us (43%)
  other arithmetic  121 us (20%)
  blocking collectives  85.5 us (14%)
  matrix products  66.2 us (11%)
  local copies, waits for them, and re-layouts  49.1 us (8%)
  between operations  16 us (3%)
  starting transfers between devices  7.05 us (1%)
    psum x1, waiting for transfers between devices, shards(): branch = lax.psum(partial_out, 'head').reshape(seq_count, blk_rows, width)  109 us
    psum x1, waiting for transfers between devices, shards(): lax.psum((g_ngain, g_in, g_taps, g_heads, g_ggain, g_out), 'seq')  100 us
    another operation x7, other arithmetic  40.2 us
    psum x1, blocking collectives, shards(): lax.psum((g_ngain, g_in, g_taps, g_heads, g_ggain, g_out), 'seq')  39.4 us
    all_gather x1, waiting for transfers between devices, prefix_2(): lax.all_gather(part.astype(kind), axis)  28 us
    dot_general x3, matrix products, span_parts(): jnp.einsum('tsh,shp->thp', weights, step_sizes[:, :, None] * x_values, pr...  27.7 us
    all_gather x1, blocking collectives, prefix_2(): lax.all_gather(part.astype(kind), axis)  26.7 us
    all_gather x1, waiting for transfers between devices, entering(): lax.all_gather(a.astype(kind), axis)  25.6 us
  transfers between devices with their start and end apart: 7, of which 4 were waited for; matrix products, arithmetic and copies ran while one was open for 21% of the time, Pallas kernels for 0%

commit v1 on v0

v1 whole, which is shorter than its diff:
```python
import functools
import math

import jax
import jax.numpy as jnp
from jax import lax
from jax.experimental import pallas as pl
from jax.experimental.pallas import tpu as pltpu
from jax.sharding import PartitionSpec as P

HDIM = 64
CONV = 4
INNER = 1536
EPSILON = 1e-05
MOMENTUM = 0.5
AVERAGE = 0.5
RATES = (0.15, 0.1, 0.5, 0.05, 0.15, 0.02)
HIGHEST = lax.Precision.HIGHEST
F32 = jnp.float32
BF16 = jnp.bfloat16
GRP = 4
BLK = 256
HALF = BLK // 2
QUART = BLK // 4
D = 768
ZW = 384
NH = 6
ST = 128
SW = 32
LANES = 128
WCOLS = D // LANES
WROWS = 2 * ZW + 2 * SW
TOK = GRP * BLK
COLS = WROWS + NH
SEG1 = 2 * ZW // GRP
SEG2 = 120
BC_AT, DT_AT, TAP_AT, HD_AT, GG_AT, NG_AT = 384, 448, 456, 464, 472, 473


def nt(a, b, precision=None):
    return lax.dot_general(
        a, b, (((1,), (1,)), ((), ())), preferred_element_type=F32, precision=precision
    )


def nn(a, b, precision=None):
    return lax.dot_general(
        a, b, (((1,), (0,)), ((), ())), preferred_element_type=F32, precision=precision
    )


def tn(a, b, precision=None):
    return lax.dot_general(
        a, b, (((0,), (0,)), ((), ())), preferred_element_type=F32, precision=precision
    )


def iota(shape, dim):
    return lax.broadcasted_iota(jnp.int32, shape, dim)


def spread(kind):
    return (iota((LANES, ZW), 0) == iota((LANES, ZW), 1) // HDIM + 8 * kind).astype(F32)


def gather_heads():
    return (iota((ZW, LANES), 1) == iota((ZW, LANES), 0) // HDIM).astype(F32)


def wide(packed, kind):
    return nn(packed, spread(kind), HIGHEST)


def head_sums(values):
    return nn(values, gather_heads(), HIGHEST)


def lane_mask(which):
    return (iota((1, LANES), 1) // HDIM == which).astype(BF16)


def lower_triangle():
    return (iota((BLK, BLK), 0) >= iota((BLK, BLK), 1)).astype(F32)


def call(kernel, name, grid, ins, in_specs, outs, out_specs, scratch=(), prefetch=None, flops=0, aliases=None):
    params = pltpu.CompilerParams(
        dimension_semantics=("arbitrary",) * len(grid), vmem_limit_bytes=40 << 20
    )
    nbytes = sum(math.prod(a.shape) * a.dtype.itemsize for a in ins)
    nbytes += sum(math.prod(a.shape) * a.dtype.itemsize for a in outs)
    cost = pl.CostEstimate(flops=flops, bytes_accessed=nbytes, transcendentals=0)
    spec = pltpu.PrefetchScalarGridSpec(
        num_scalar_prefetch=0 if prefetch is None else 1,
        grid=grid,
        in_specs=in_specs,
        out_specs=out_specs,
        scratch_shapes=scratch,
    )
    return pl.pallas_call(
        kernel,
        grid_spec=spec,
        out_shape=outs,
        compiler_params=params,
        cost_estimate=cost,
        input_output_aliases=aliases or {},
        name=name,
    )(*(() if prefetch is None else (prefetch,)), *ins)


def sds(shape, dtype=F32):
    return jax.ShapeDtypeStruct(shape, dtype)


def whole(shape):
    return pl.BlockSpec(shape, lambda *_: (0,) * len(shape))


def rows(width, height=BLK):
    return pl.BlockSpec((height, width), lambda i, *_: (i, 0))


def rows_back(width, height=BLK):
    return pl.BlockSpec((height, width), lambda i, *_: (GRP - 1 - i, 0))


def slot(height, width=D):
    return pl.BlockSpec((1, height, width), lambda i, at: (i ^ at[0], 0, 0))


def pick_kernel(at, *refs):
    for source, goal in zip(refs[:GRP], refs[GRP : 2 * GRP]):
        goal[...] = source[0]


def pick(at, array, after=()):
    def half_of(b):
        return pl.BlockSpec((1, HALF, D), lambda i, at: (at[0] ^ b, at[1], 0))

    def kernel(at, *refs):
        pick_kernel(at, *refs[:GRP], *refs[GRP + len(after) :])

    tokens = [pl.BlockSpec(memory_space=pl.ANY)] * len(after)
    return call(
        kernel, "pick", (1,), (array,) * GRP + tuple(after), [half_of(b) for b in range(GRP)] + tokens,
        [sds((HALF, D), BF16)] * GRP, [whole((HALF, D))] * GRP, prefetch=at,
    )


def prep_kernel(win, wout, taps, w_ref, wdt_ref, low_ref, send_ref, wide_w, sem):
    copy = pltpu.make_async_copy(win.at[:, 0, :], wide_w, sem)
    copy.start()
    low_ref[...] = wout[...].astype(BF16)
    copy.wait()
    w_ref[...] = wide_w[0:WROWS, :].astype(BF16)
    last = jnp.concatenate([wide_w[WROWS:, :], jnp.zeros((8 - NH, D), F32)], axis=0)
    wdt_ref[...] = jnp.concatenate([last] * 16, axis=0).astype(BF16)
    send_ref[0 : 2 * SW, :] = w_ref[2 * ZW : WROWS, :]
    own = taps[:, 0, :][:, ZW:]
    high = own.astype(BF16).astype(F32)
    mid = (own - high).astype(BF16).astype(F32)
    low = own - high - mid
    parts = jnp.concatenate([high, mid, low, jnp.zeros((1, 2 * SW), F32)], axis=0)
    send_ref[2 * SW :, :] = jnp.zeros((16, D), BF16)
    send_ref[2 * SW :, 0 : 2 * SW] = parts.astype(BF16)


def chunk_of(own_ref, oth_ref, core):
    own, oth = own_ref[0], oth_ref[0]
    first = core == 0
    return jnp.concatenate([jnp.where(first, own, oth), jnp.where(first, oth, own)], axis=0)


def normalise(x, gain):
    u = x.astype(F32)
    scale = lax.rsqrt(jnp.mean(u * u, axis=-1, keepdims=True) + EPSILON)
    return (u * scale * gain).astype(BF16)


def first_kernel(at, own, oth, gain, wz, wdt, hp, nrm_ref, z_ref, info_ref, row_ref, tot_ref, cum):
    step = pl.program_id(0)

    @pl.when(step == 0)
    def _():
        cum[...] = jnp.zeros_like(cum)

    normed = normalise(chunk_of(own, oth, at[1]), gain[...])
    nrm_ref[...] = normed
    z_ref[...] = nt(normed, wz[...])
    biased = nt(normed, wdt[...]) + hp[0:1, :]
    steps = jax.nn.softplus(biased)
    decays = -jnp.exp(hp[1:2, :]) * steps
    c = nn(lower_triangle(), decays, HIGHEST)
    base = cum[0:1, :]
    group = iota((BLK, LANES), 1) // 8
    info = jnp.where(group == 0, c, jnp.where(group == 1, steps, biased))
    info_ref[...] = jnp.where(group == 3, base + c, info)
    row_ref[...] = jnp.transpose(c)[0:8, :]
    cum[0:1, :] = base + c[BLK - 1 : BLK, :]
    tot_ref[...] = jnp.broadcast_to(cum[0:1, :], (8, LANES))


def mix_kernel(
    nrm, halo, gain, wx, wo, bc0, bc1, bc2, bc3, taps, info,
    mx_ref, px_ref, xa_ref, xdt_ref, mo_ref, po_ref, b_ref, c_ref, h_ref, s_ref,
    wbc, tbc, ext, exto, state,
):
    step = pl.program_id(0)
    tap = taps[:, 0, :]

    @pl.when(step == 0)
    def _():
        place = jnp.zeros((16, 2 * ST), F32)
        for b, buf in enumerate((bc0, bc1, bc2, bc3)):
            wbc[SW * b : SW * (b + 1), :] = buf[0:SW, :]
            wbc[ST + SW * b : ST + SW * (b + 1), :] = buf[SW : 2 * SW, :]
            at_row, at_col = iota((2 * SW, 2 * ST), 0), iota((2 * SW, 2 * ST), 1)
            goal = jnp.where(at_row < SW, SW * b + at_row, ST + SW * b + at_row - SW)
            put = (at_col == goal).astype(BF16)
            place = place + nn(buf[2 * SW :, 0 : 2 * SW], put)
        tbc[0:5, :] = place[0:5] + place[5:10] + place[10:15]
        before = normalise(halo[...], gain[...])
        ext[0:8, 0:ZW] = nt(before, wx[...])[8:16]
        ext[0:8, ZW:] = nt(before, wbc[...])[8:16]
        exto[0:8, :] = nt(before, wo[...])[8:16]
        state[...] = jnp.zeros_like(state)

    normed = nrm[...]
    mixed = nt(normed, wx[...])
    mx_ref[...] = mixed
    ext[8:, 0:ZW] = mixed
    ext[8:, ZW:] = nt(normed, wbc[...])
    own = nt(normed, wo[...])
    mo_ref[...] = own
    exto[8:, :] = own
    pre = tap[4:5, 0:ZW]
    pre_bc = tbc[4:5, :]
    pre_o = tap[4:5, ZW:]
    for k in range(CONV):
        pre = pre + tap[k : k + 1, 0:ZW] * ext[5 + k : 5 + k + BLK, 0:ZW]
        pre_bc = pre_bc + tbc[k : k + 1, :] * ext[5 + k : 5 + k + BLK, ZW:]
        pre_o = pre_o + tap[k : k + 1, ZW:] * exto[5 + k : 5 + k + BLK, :]
    px_ref[...] = pre
    po_ref[...] = pre_o
    x = pre * jax.nn.sigmoid(pre)
    xa_ref[...] = x
    bc = (pre_bc * jax.nn.sigmoid(pre_bc)).astype(BF16)
    b_ref[...] = bc[:, 0:ST]
    c_ref[...] = bc[:, ST:]
    ext[0:8, :] = ext[BLK:, :]
    exto[0:8, :] = exto[BLK:, :]

    packed = info[...]
    c = packed[:, 0:LANES]
    keep = iota((BLK, LANES), 1) < 8
    tail = jnp.where(keep, jnp.exp(jnp.where(keep, c[BLK - 1 : BLK, :] - c, 0.0)), 0.0)
    xdt = x * wide(packed, 1)
    xdt_ref[...] = xdt.astype(BF16)
    fresh = tn((xdt * wide(tail, 0)).astype(BF16), bc[:, 0:ST])
    h_ref[0] = state[...]
    for h in range(NH):
        decay = jnp.exp(packed[BLK - 1 : BLK, h : h + 1])
        at = pl.ds(HDIM * h, HDIM)
        state[at, :] = decay * state[at, :] + fresh[HDIM * h : HDIM * (h + 1), :]
    s_ref[...] = state[...].astype(BF16)


def weights_of(h, packed, row, causal):
    diff = packed[:, h : h + 1] - row[h : h + 1, :]
    return jnp.where(causal, jnp.exp(jnp.where(causal, diff, 0.0)), 0.0)


def local_kernel(
    at, xdt, xa, b, c, info, row, hloc, own, oth, low, skip, yl_ref, dyn_ref, w_ref
):
    step = pl.program_id(0)
    packed = info[...]
    rowc = row[...]
    causal = iota((BLK, BLK), 0) >= iota((BLK, BLK), 1)
    scores = nt(c[...], b[...])
    c_exp = jnp.exp(jnp.where(iota((BLK, LANES), 1) < 8, packed, 0.0))
    carried = nt(c[...], hloc[0].astype(BF16)) * wide(c_exp, 0)
    carried = carried + skip[0:1, :] * xa[...]
    for p in range(NH // 2):
        x = xdt[:, LANES * p : LANES * (p + 1)]
        total = carried[:, LANES * p : LANES * (p + 1)]
        for q in range(2):
            weights = (weights_of(2 * p + q, packed, rowc, causal) * scores).astype(BF16)
            total = total + nn(weights, x * lane_mask(q))
        yl_ref[:, LANES * p : LANES * (p + 1)] = total
    place = (at[2] * GRP + step) * BLK + iota((BLK, 1), 0)
    live = place < at[3]
    w = jnp.where(live, chunk_of(own, oth, at[1]), 0.0).astype(BF16)
    w_ref[...] = w
    dyn_ref[...] = nt(w, low[...])


def gate_kernel(yl, c, info, hin, z, dyn, gg, y_ref, sum_ref):
    packed = info[...]
    lane = iota((BLK, LANES), 1)
    cum = jnp.where(lane // 8 == 3, jnp.exp(jnp.where(lane // 8 == 3, packed, 0.0)), 0.0)
    y = yl[...] + nt(c[...], hin[...]) * wide(cum, 3)
    y_ref[...] = y
    gate = z[...]
    g = y * (gate * jax.nn.sigmoid(gate))
    squares = jnp.sum(g * g, axis=-1, keepdims=True)
    inner = jnp.sum(dyn[...] * gg[...] * g, axis=-1, keepdims=True)
    both = jnp.where(lane == 0, squares, jnp.where(lane == 1, inner, 0.0))
    sum_ref[...] = jnp.transpose(both)[0:8, :]


def ungate_kernel(
    y, z, dyn, s0, s1, s2, s3, info, c, gg, dy_ref, dz_ref, yn_ref, p_ref, gg_ref, acc
):
    step = pl.program_id(0)

    @pl.when(step == 0)
    def _():
        acc[...] = jnp.zeros_like(acc)
        gg_ref[...] = jnp.zeros_like(gg_ref)

    sums = s0[...] + s1[...] + s2[...] + s3[...]
    sums = jnp.transpose(jnp.concatenate([sums, jnp.zeros((LANES - 8, BLK), F32)], axis=0))
    q = lax.rsqrt(sums[:, 0:1] / INNER + EPSILON)
    mean = sums[:, 1:2] * q / INNER
    gate = z[...]
    sigma = jax.nn.sigmoid(gate)
    silu = gate * sigma
    out = y[...]
    g = out * silu
    n = g * q
    d = dyn[...]
    d_g = q * (d * gg[...] - n * mean)
    d_y = d_g * silu
    dy_ref[...] = d_y
    dz_ref[...] = (d_g * out * sigma * (1.0 + gate * (1.0 - sigma))).astype(BF16)
    yn_ref[...] = (n * gg[...]).astype(BF16)
    gg_ref[0:1, :] += jnp.sum(d * n, axis=0, keepdims=True)
    packed = info[...]
    lane = iota((BLK, LANES), 1)
    cum = jnp.where(lane // 8 == 3, jnp.exp(jnp.where(lane // 8 == 3, packed, 0.0)), 0.0)
    acc[...] += tn((d_y * wide(cum, 3)).astype(BF16), c[...])
    p_ref[...] = acc[...].astype(BF16)


def halves(value, core, keep_ref, send_ref):
    low, high = value[0:HALF], value[HALF:]
    first = core == 0
    keep_ref[0] = jnp.where(first, low, high)
    send_ref[0] = jnp.where(first, high, low)


def out_kernel(
    at, yn, w, low, nrm, dz, keep_ref, send_ref, g0, g1, g2, g3, acc
):
    step = pl.program_id(0)

    @pl.when(step == 0)
    def _():
        acc[...] = jnp.zeros_like(acc)

    halves(nn(yn[...], low[...]).astype(BF16), at[1], keep_ref, send_ref)
    acc[0:ZW, :] += tn(dz[...], nrm[...])
    acc[ZW:, :] += tn(yn[...], w[...])

    @pl.when(step == GRP - 1)
    def _():
        for b, ref in enumerate((g0, g1, g2, g3)):
            start = pl.multiple_of((at[0] ^ b) * SEG1, SEG1)
            ref[...] = acc[pl.ds(start, SEG1), :].astype(BF16)


def inner_kernel(
    xdt, b, c, info, row, dy, hloc, hin, token, dxi_ref, dbi_ref, dci_ref, dcum_ref, hall_ref
):
    packed = info[...]
    rowc = row[...]
    lane = iota((BLK, LANES), 1)
    causal = iota((BLK, BLK), 0) >= iota((BLK, BLK), 1)
    bb, cc = b[...], c[...]
    scores = nt(cc, bb)
    d_scores = jnp.zeros((BLK, BLK), F32)
    d_cum = jnp.zeros((BLK, LANES), F32)
    columns = []
    dyv = dy[...]
    for p in range(NH // 2):
        x = xdt[:, LANES * p : LANES * (p + 1)]
        d = dyv[:, LANES * p : LANES * (p + 1)].astype(BF16)
        total = jnp.zeros((BLK, LANES), F32)
        for q in range(2):
            h = 2 * p + q
            spans = weights_of(h, packed, rowc, causal)
            d_h = d * lane_mask(q)
            d_spans = nt(d_h, x) * spans
            d_scores = d_scores + d_spans
            both = d_spans * scores
            d_cum = d_cum + jnp.where(lane == h, jnp.sum(both, axis=1, keepdims=True), 0.0)
            columns.append(jnp.sum(both, axis=0, keepdims=True))
            total = total + tn((spans * scores).astype(BF16), d_h)
        dxi_ref[:, LANES * p : LANES * (p + 1)] = total
    columns = jnp.concatenate(columns + [jnp.zeros((LANES - NH, BLK), F32)], axis=0)
    d_cum = d_cum - jnp.transpose(columns)
    low_scores = d_scores.astype(BF16)
    c_exp = jnp.exp(jnp.where(lane < 8, packed, 0.0))
    c_wide = wide(c_exp, 0)
    base = packed[0:1, 24:32] - packed[0:1, 0:8]
    for h in range(NH):
        at = pl.ds(HDIM * h, HDIM)
        grown = jnp.exp(base[:, h : h + 1]) * hin[at, :].astype(F32)
        hall_ref[0, at, :] = hloc[0, at, :] + grown
    entering = hall_ref[0].astype(BF16)
    carried = nt(cc, entering) * c_wide
    d_cum = d_cum + head_sums(dyv * carried)
    dcum_ref[...] = d_cum
    dci_ref[...] = nn(low_scores, bb) + nn((dyv * c_wide).astype(BF16), entering)
    dbi_ref[...] = tn(low_scores, cc)


def back_kernel(
    after, dxi, dbi, dci, dcum, hall, xa, px, b, c, info, dy, hp, skip,
    dpx_ref, o0, o1, o2, o3, draw_ref, hg_ref, state,
):
    step = pl.program_id(0)

    @pl.when(step == 0)
    def _():
        state[...] = after[...].astype(F32)
        hg_ref[...] = jnp.zeros_like(hg_ref)

    packed = info[...]
    lane = iota((BLK, LANES), 1)
    first = lane < 8
    c_last = packed[BLK - 1 : BLK, :]
    tail = jnp.where(first, jnp.exp(jnp.where(first, c_last - packed, 0.0)), 0.0)
    c_exp = jnp.exp(jnp.where(first, packed, 0.0))
    tail_wide, c_wide, dt_wide = wide(tail, 0), wide(c_exp, 0), wide(packed, 1)
    x = xa[...]
    xdt = x * dt_wide
    d_y = dy[...]
    bb, cc = b[...], c[...]
    low_state = state[...].astype(BF16)
    d_tail = nt(bb, low_state) * tail_wide
    tails = head_sums(xdt * d_tail)
    d_xdt = dxi[...] + d_tail
    d_b = dbi[...] + nn((xdt * tail_wide).astype(BF16), low_state)
    d_c = dci[...]
    ending = jnp.sum(tails, axis=0, keepdims=True)
    lane1 = iota((1, LANES), 1)
    for h in range(NH):
        at = pl.ds(HDIM * h, HDIM)
        inner = jnp.sum(state[at, :] * hall[0, at, :], axis=(0, 1), keepdims=True)
        ending = ending + jnp.where(lane1 == h, inner * jnp.exp(c_last[:, h : h + 1]), 0.0)
    d_cum = dcum[...] - tails
    d_cum = d_cum + jnp.where(iota((BLK, LANES), 0) == BLK - 1, ending, 0.0)
    d_a = tn(lower_triangle(), d_cum, HIGHEST)
    fresh = tn((d_y * c_wide).astype(BF16), cc)
    for h in range(NH):
        at = pl.ds(HDIM * h, HDIM)
        decay = jnp.exp(c_last[:, h : h + 1])
        state[at, :] = decay * state[at, :] + fresh[HDIM * h : HDIM * (h + 1), :]
    rate = -jnp.exp(hp[1:2, :])
    d_dt = head_sums(x * d_xdt) + rate * d_a
    biased = pltpu.roll(packed, LANES - 16, 1)
    steps = pltpu.roll(packed, LANES - 8, 1)
    used = lane < NH
    d_raw = jnp.where(used, d_dt * jax.nn.sigmoid(jnp.where(used, biased, 0.0)), 0.0)
    draw_ref[...] = d_raw.astype(BF16)
    hg_ref[0:1, :] += jnp.sum(d_raw, axis=0, keepdims=True)
    g_rate = jnp.where(used, d_a * rate * jnp.where(used, steps, 0.0), 0.0)
    hg_ref[1:2, :] += jnp.sum(g_rate, axis=0, keepdims=True)
    hg_ref[2:3, :] += jnp.sum(head_sums(d_y * x), axis=0, keepdims=True)
    d_x = d_xdt * dt_wide + skip[0:1, :] * d_y
    pre = px[...]
    sigma = jax.nn.sigmoid(pre)
    dpx_ref[...] = d_x * sigma * (1.0 + pre * (1.0 - sigma))
    for s, ref in enumerate((o0, o1, o2, o3)):
        ref[:, 0:SW] = d_b[:, SW * s : SW * (s + 1)].astype(BF16)
        ref[:, SW:] = d_c[:, SW * s : SW * (s + 1)].astype(BF16)


def edge_kernel(o0, r1, r2, r3, po, dpx, dpo_ref, halo_ref):
    d = o0[...].astype(F32) + r1[...].astype(F32) + r2[...].astype(F32) + r3[...].astype(F32)
    pre = po[...]
    sigma = jax.nn.sigmoid(pre)
    d = d * sigma * (1.0 + pre * (1.0 - sigma))
    dpo_ref[...] = d

    @pl.when(pl.program_id(0) == 0)
    def _():
        halo_ref[:, 0:ZW] = dpx[0:8, :]
        halo_ref[:, ZW:] = jnp.zeros((8, LANES), F32)
        halo_ref[:, ZW : ZW + 2 * SW] = d[0:8, :]


def last_kernel(
    at, dpx, dpo, halo, mx, mo, taps, dz, draw, nrm, w, wdt, gain, gg, hg,
    keep_ref, send_ref, g0, g1, g2, g3,
    ext, exto, acc, acc_t, acc_n, tap_x, tap_o,
):
    step = pl.program_id(0)
    tap = taps[:, 0, :]

    @pl.when(step == 0)
    def _():
        ext[BLK:, :] = halo[:, 0:ZW]
        exto[BLK:, :] = halo[:, ZW : ZW + 2 * SW]
        for ref in (acc, acc_t, acc_n, tap_x, tap_o):
            ref[...] = jnp.zeros_like(ref)

    d_x, d_o = dpx[...], dpo[...]
    ext[0:BLK, :] = d_x
    exto[0:BLK, :] = d_o
    d_mx = jnp.zeros((BLK, ZW), F32)
    d_mo = jnp.zeros((BLK, 2 * SW), F32)
    for k in range(CONV):
        d_mx = d_mx + tap[k : k + 1, 0:ZW] * ext[3 - k : 3 - k + BLK, :]
        d_mo = d_mo + tap[k : k + 1, ZW:] * exto[3 - k : 3 - k + BLK, :]
    v_x, v_o = mx[...], mo[...]
    for k in range(CONV):
        tap_x[k : k + 1, :] += jnp.sum(v_x * ext[3 - k : 3 - k + BLK, :], axis=0, keepdims=True)
        tap_o[k : k + 1, :] += jnp.sum(v_o * exto[3 - k : 3 - k + BLK, :], axis=0, keepdims=True)
    tap_x[4:5, :] += jnp.sum(d_x, axis=0, keepdims=True)
    tap_o[4:5, :] += jnp.sum(d_o, axis=0, keepdims=True)
    ext[BLK:, :] = d_x[0:8]
    exto[BLK:, :] = d_o[0:8]
    p_x, p_o = d_mx.astype(BF16), d_mo.astype(BF16)
    p_z, p_t = dz[...], draw[...]
    back = nn(p_z, w[0:ZW, :]) + nn(p_x, w[ZW : 2 * ZW, :])
    back = back + nn(p_o, w[2 * ZW : WROWS, :]) + nn(p_t, wdt[...])
    halves(back.astype(BF16), at[1], keep_ref, send_ref)
    normed = nrm[...]
    acc_n[0:1, :] += jnp.sum(back * normed.astype(F32), axis=0, keepdims=True)
    acc[0:ZW, :] += tn(p_x, normed)
    acc[BC_AT:DT_AT, :] += tn(p_o, normed)
    acc_t[...] += tn(p_t, normed)

    @pl.when(step == GRP - 1)
    def _():
        acc[DT_AT:, :] = jnp.zeros((GRP * SEG2 - DT_AT, D), F32)
        acc[DT_AT : DT_AT + NH, :] = acc_t[0:NH, :]
        acc[TAP_AT : TAP_AT + 5, 0:ZW] = tap_x[0:5, :]
        acc[TAP_AT : TAP_AT + 5, ZW : ZW + 2 * SW] = tap_o[0:5, :]
        acc[HD_AT : HD_AT + 8, 0:LANES] = hg[...]
        acc[GG_AT : GG_AT + 1, 0:ZW] = gg[0:1, :]
        acc[NG_AT : NG_AT + 1, :] = acc_n[0:1, :] / gain[...]
        for b, ref in enumerate((g0, g1, g2, g3)):
            start = pl.multiple_of((at[0] ^ b) * SEG2, 8)
            ref[...] = acc[pl.ds(start, SEG2), :].astype(BF16)


def split_kernel(at, keep, other, keep_ref, send_ref):
    value = keep[0].astype(F32) + other[0].astype(F32)
    low, high = value[0:QUART], value[QUART:]
    first = at[4] == 0
    keep_ref[0] = jnp.where(first, low, high)
    send_ref[0] = jnp.where(first, high, low).astype(BF16)


def add_kernel(keep, other, r0, r1, r2, r3):
    for b, ref in enumerate((r0, r1, r2, r3)):
        ref[...] = (keep[b] + other[b].astype(F32)).astype(BF16)


def sum_kernel(*refs):
    total = refs[0][...].astype(F32)
    for ref in refs[1:-1]:
        total = total + ref[...].astype(F32)
    refs[-1][...] = total.astype(refs[-1].dtype)


def place_quarters(at, b, parts, scr):
    core, xbit = at[1], at[4]
    for n, ref in enumerate(parts):
        half = core if n < 2 else 1 - core
        quarter = xbit if n % 2 == 0 else 1 - xbit
        start = pl.multiple_of(half * HALF + quarter * QUART, QUART)
        scr[pl.ds(start, QUART), :] = ref[0]


def home_out_kernel(at, lens, block, a, x, ac, xc, out_ref, scr):
    step = pl.program_id(0)
    place_quarters(at, step, (a, x, ac, xc), scr)
    place = (at[2] * GRP + at[0]) * BLK + iota((BLK, 1), 0)
    live = place < lens[step]
    total = block[0].astype(F32) + scr[...].astype(F32)
    out_ref[0] = jnp.where(live, total, 0.0).astype(BF16)


def home_grad_kernel(at, lens, block, cot, gain, a, x, ac, xc, out_ref, scr):
    step = pl.program_id(0)
    place_quarters(at, step, (a, x, ac, xc), scr)
    place = (at[2] * GRP + at[0]) * BLK + iota((BLK, 1), 0)
    live = place < lens[step]
    u = block[0].astype(F32)
    scale = lax.rsqrt(jnp.mean(u * u, axis=-1, keepdims=True) + EPSILON)
    m = u * scale
    f = scr[...].astype(F32) * gain[...]
    inner = jnp.mean(f * m, axis=-1, keepdims=True)
    out_ref[0] = scale * (f - m * inner) + jnp.where(live, cot[0].astype(F32), 0.0)


def home(kernel, name, at, lens, arrays, specs, parts, dtype):
    full = pl.BlockSpec((1, BLK, D), lambda i, *_: (i, 0, 0))
    part = pl.BlockSpec((1, QUART, D), lambda i, at, lens: (i ^ at[0], 0, 0))
    specs = [full if s is None else whole(s) for s in specs]
    spec = pltpu.PrefetchScalarGridSpec(
        num_scalar_prefetch=2,
        grid=(GRP,),
        in_specs=specs + [part] * 4,
        out_specs=full,
        scratch_shapes=[pltpu.VMEM((BLK, D), BF16)],
    )
    return pl.pallas_call(
        kernel,
        grid_spec=spec,
        out_shape=sds((GRP, BLK, D), dtype),
        cost_estimate=pl.CostEstimate(flops=0, bytes_accessed=8 << 20, transcendentals=0),
        name=name,
    )(at, lens, *arrays, *parts)


def advance(weight, gradient, moment, average, rate):
    moment_new = MOMENTUM * moment + gradient
    weight_new = weight - rate * (gradient + MOMENTUM * moment_new)
    average_new = AVERAGE * average + (1.0 - AVERAGE) * weight_new
    return (weight_new, moment_new, average_new)


def stepped(grad_of, weights, outs, blocks, buffers, sems, rate):
    ins, done = buffers[:3], buffers[3:]

    def reads(n):
        start, size = blocks[n]
        return [
            pltpu.make_async_copy(
                w.at[pl.ds(start, size), 0, :], buf.at[pl.ds(start, size), :], sems.at[n, j]
            )
            for j, (w, buf) in enumerate(zip(weights, ins))
        ]

    def writes(n):
        start, size = blocks[n]
        return [
            pltpu.make_async_copy(
                buf.at[pl.ds(start, size), :], o.at[pl.ds(start, size), 0, :], sems.at[n, 3 + j]
            )
            for j, (o, buf) in enumerate(zip(outs, done))
        ]

    for n in range(len(blocks)):
        for copy in reads(n):
            copy.start()
    for n, (start, size) in enumerate(blocks):
        for copy in reads(n):
            copy.wait()
        here = pl.ds(start, size)
        new = advance(ins[0][here, :], grad_of(n), ins[1][here, :], ins[2][here, :], rate)
        for buf, value in zip(done, new):
            buf[here, :] = value
        for copy in writes(n):
            copy.start()
    for n in range(len(blocks)):
        for copy in writes(n):
            copy.wait()


Z_BLOCKS = tuple((96 * n, 96) for n in range(4))
X_BLOCKS = tuple((ZW + 96 * n, 96) for n in range(4)) + ((2 * ZW, COLS - 2 * ZW),)


def update_a_kernel(
    at, g0, g1, g2, g3, w, m, a, wi, mi, ai, w_ref, m_ref, a_ref, wo, mo, ao,
    grad, b0, b1, b2, b3, b4, b5, sems, *, rate, rate_in,
):
    for b, ref in enumerate((g0, g1, g2, g3)):
        grad[pl.ds(pl.multiple_of((at[0] ^ b) * SEG1, SEG1), SEG1), :] = ref[...].astype(F32)
    stepped(
        lambda n: grad[96 * n : 96 * (n + 1), :], (wi, mi, ai), (wo, mo, ao), Z_BLOCKS,
        (b0, b1, b2, b3, b4, b5), sems, rate_in,
    )
    w_ref[...], m_ref[...], a_ref[...] = advance(w[...], grad[ZW:, :], m[...], a[...], rate)


def update_b_kernel(
    at, g0, g1, g2, g3, wi, mi, ai, x0, x1, x2, wo, mo, ao, small_ref,
    grad, b0, b1, b2, b3, b4, b5, sems, *, rate,
):
    for b, ref in enumerate((g0, g1, g2, g3)):
        start = pl.multiple_of((at[0] ^ b) * SEG2, 8)
        grad[pl.ds(start, SEG2), :] = ref[...].astype(F32)
    stepped(
        lambda n: grad[96 * n : min(96 * (n + 1), COLS - ZW), :], (wi, mi, ai), (wo, mo, ao), X_BLOCKS,
        (b0, b1, b2, b3, b4, b5), sems, rate,
    )
    small_ref[...] = grad[TAP_AT : TAP_AT + 24, :]


def trade(axis, flip):
    count = lax.axis_size(axis)
    pairs = [(i, i ^ flip) for i in range(count)]
    return lambda array: lax.ppermute(array, axis, pairs)


def moved(array, by):
    count = lax.axis_size("seq")
    pairs = [(i, i + by) for i in range(count) if 0 <= i + by < count]
    return lax.ppermute(array, "seq", pairs)


def grow(decay, state):
    return jnp.repeat(decay[0, 0:NH], HDIM)[:, None] * state


def pieces_before(state, logs, way):
    count = lax.axis_size("seq") // GRP
    found = moved(state, way * GRP)
    by = 1
    if count > 2:
        there = lax.axis_index("seq") // GRP
        decay = moved(jnp.exp(logs), way * GRP)
        total = found.astype(F32)
        while by < count - 1:
            inside = (there >= by) if way > 0 else (there + by < count)
            earlier = moved(total.astype(BF16), way * GRP * by).astype(F32)
            total = jnp.where(inside, grow(decay, earlier) + total, total)
            decay = decay * moved(decay, way * GRP * by)
            by *= 2
        found = total.astype(BF16)
    return found


def summed_over_seq(parts, height):
    got = [trade("seq", b)(parts[b]) for b in (1, 2, 3)]
    spec = whole((height, D))

    def add(*arrays):
        specs = [spec] * len(arrays)
        out = [sds((height, D), BF16)]
        return call(sum_kernel, "sum", (1,), arrays, specs, out, [spec])[0]

    mine = add(parts[0], *got)
    by = GRP
    while by < lax.axis_size("seq"):
        mine = add(mine, trade("seq", by)(mine))
        by *= 2
    return [mine] + [trade("seq", b)(mine) for b in (1, 2, 3)]


def returned(at, keep, send):
    slot3 = lambda height: pl.BlockSpec((1, height, D), lambda i, at: (i, 0, 0))
    other = trade("head", 1)(send)
    keep2, send2 = call(
        split_kernel, "split", (GRP,), (keep, other), [slot3(HALF)] * 2,
        [sds((GRP, QUART, D)), sds((GRP, QUART, D), BF16)], [slot3(QUART)] * 2, prefetch=at,
    )
    other2 = trade("head", 2)(send2)
    every = whole((GRP, QUART, D))
    parts = call(
        add_kernel, "add", (1,), (keep2, other2), [every] * 2,
        [sds((QUART, D), BF16)] * 4, [whole((QUART, D))] * 4,
    )
    got = [parts[0]] + [trade("seq", b)(parts[b]) for b in (1, 2, 3)]
    a = jnp.stack(got)
    x = trade("head", 2)(a)
    return a, x, trade("head", 1)(a), trade("head", 1)(x)


def shards(
    block_in, cotangent, lengths,
    norm_gain, in_proj, conv_params, head_params, gate_gain, out_proj,
    norm_gain_momentum, in_proj_momentum, conv_momentum, head_momentum, gate_gain_momentum,
    out_proj_momentum,
    norm_gain_average, in_proj_average, conv_average, head_average, gate_gain_average,
    out_proj_average,
):
    seq_at, head_at = lax.axis_index("seq"), lax.axis_index("head")
    place = seq_at % GRP
    at = jnp.stack([place, head_at % 2, seq_at // GRP, lengths[place], head_at // 2])
    at = at.astype(jnp.int32)
    gain = norm_gain.reshape(1, D)
    ggain = gate_gain.reshape(1, ZW)
    hp = jnp.tile(jnp.pad(head_params, ((0, 5), (0, 2))), (1, 16))
    skip = jnp.repeat(head_params[2], HDIM).reshape(1, ZW)

    def turned(array):
        return jnp.transpose(array, (2, 1, 0))

    anyspec = pl.BlockSpec(memory_space=pl.ANY)
    picked = pick(at, block_in)
    got = [picked[0]] + [trade("seq", b)(picked[b]) for b in (1, 2, 3)]
    w, wdt, low, send_bc = call(
        prep_kernel, "prep", (1,), (turned(in_proj), out_proj, conv_params),
        [anyspec, whole((ZW, D)), whole((5, 1, 448))],
        [sds((WROWS, D), BF16), sds((LANES, D), BF16), sds((ZW, D), BF16), sds((80, D), BF16)],
        [whole((WROWS, D)), whole((LANES, D)), whole((ZW, D)), whole((80, D))],
        scratch=[pltpu.VMEM((COLS, D), F32), pltpu.SemaphoreType.DMA],
    )
    bcs = [send_bc] + [trade("head", b)(send_bc) for b in (1, 2, 3)]
    own = jnp.stack(got)
    oth = trade("head", 1)(own)
    high = jnp.where(head_at % 2 == 1, own[:, HALF - 16 :], oth[:, HALF - 16 :])
    edge = lax.dynamic_index_in_dim(high, place ^ (GRP - 1), 0, False)
    halo = moved(edge, GRP)
    cot_picked = pick(at, cotangent, (own,))
    cot_got = [cot_picked[0]] + [trade("seq", b)(cot_picked[b]) for b in (1, 2, 3)]
    cot_own = jnp.stack(cot_got)
    cot_oth = trade("head", 1)(cot_own)

    def wblock(n, height):
        return pl.BlockSpec((height, D), lambda i, *_: (n, 0))

    nrm, z, info, rowc, logs = call(
        first_kernel, "first", (GRP,), (own, oth, gain, w, wdt, hp),
        [slot(HALF), slot(HALF), whole((1, D)), wblock(0, ZW), whole((LANES, D)), whole((8, LANES))],
        [sds((TOK, D), BF16), sds((TOK, ZW)), sds((TOK, LANES)), sds((8, TOK)), sds((8, LANES))],
        [rows(D), rows(ZW), rows(LANES), pl.BlockSpec((8, BLK), lambda i, *_: (0, i)), whole((8, LANES))],
        scratch=[pltpu.VMEM((8, LANES), F32)], prefetch=at, flops=2 * TOK * D * 512,
    )
    hspec = pl.BlockSpec((1, ZW, ST), lambda i, *_: (i, 0, 0))
    rowspec = pl.BlockSpec((8, BLK), lambda i, *_: (0, i))
    mx, px, xa, xdt, mo, po, bb, cc, hloc, fresh = call(
        mix_kernel, "mix", (GRP,), (nrm, halo, gain, w, w, *bcs, conv_params, info),
        [rows(D), whole((16, D)), whole((1, D)), wblock(1, ZW), wblock(12, 2 * SW)]
        + [whole((80, D))] * 4 + [whole((5, 1, 448)), rows(LANES)],
        [sds((TOK, ZW)), sds((TOK, ZW)), sds((TOK, ZW)), sds((TOK, ZW), BF16), sds((TOK, 2 * SW)),
         sds((TOK, 2 * SW)), sds((TOK, ST), BF16), sds((TOK, ST), BF16), sds((GRP, ZW, ST)),
         sds((ZW, ST), BF16)],
        [rows(ZW), rows(ZW), rows(ZW), rows(ZW), rows(2 * SW), rows(2 * SW), rows(ST), rows(ST),
         hspec, whole((ZW, ST))],
        scratch=[pltpu.VMEM((2 * ST, D), BF16), pltpu.VMEM((8, 2 * ST), F32),
                 pltpu.VMEM((BLK + 8, ZW + 2 * ST), F32), pltpu.VMEM((BLK + 8, 2 * SW), F32),
                 pltpu.VMEM((ZW, ST), F32)],
        flops=2 * TOK * D * 704,
    )
    hin = pieces_before(fresh, logs, 1)
    yl, dyn, w_live = call(
        local_kernel, "local", (GRP,),
        (xdt, xa, bb, cc, info, rowc, hloc, cot_own, cot_oth, low, skip),
        [rows(ZW), rows(ZW), rows(ST), rows(ST), rows(LANES), rowspec, hspec, slot(HALF),
         slot(HALF), whole((ZW, D)), whole((1, ZW))],
        [sds((TOK, ZW)), sds((TOK, ZW)), sds((TOK, D), BF16)], [rows(ZW), rows(ZW), rows(D)],
        prefetch=at, flops=2 * TOK * (D * ZW + 4 * BLK * ZW),
    )
    y, sums = call(
        gate_kernel, "gate", (GRP,), (yl, cc, info, hin, z, dyn, ggain),
        [rows(ZW), rows(ST), rows(LANES), whole((ZW, ST)), rows(ZW), rows(ZW), whole((1, ZW))],
        [sds((TOK, ZW)), sds((8, TOK))], [rows(ZW), rowspec], flops=2 * TOK * ST * ZW,
    )
    all_sums = [sums] + [trade("head", b)(sums) for b in (1, 2, 3)]
    dy, dz, yn, pulled, g_gate = call(
        ungate_kernel, "ungate", (GRP,), (y, z, dyn, *all_sums, info, cc, ggain),
        [rows(ZW)] * 3 + [rowspec] * 4 + [rows(LANES), rows(ST), whole((1, ZW))],
        [sds((TOK, ZW)), sds((TOK, ZW), BF16), sds((TOK, ZW), BF16), sds((ZW, ST), BF16), sds((8, ZW))],
        [rows(ZW), rows(ZW), rows(ZW), whole((ZW, ST)), whole((8, ZW))],
        scratch=[pltpu.VMEM((ZW, ST), F32)], flops=2 * TOK * ST * ZW,
    )
    after = pieces_before(pulled, logs, -1)
    half_slot = pl.BlockSpec((1, HALF, D), lambda i, at: (i ^ at[0], 0, 0))
    keep, send, *grads1 = call(
        out_kernel, "out", (GRP,), (yn, w_live, low, nrm, dz),
        [rows(ZW), rows(D), whole((ZW, D)), rows(D), rows(ZW)],
        [sds((GRP, HALF, D), BF16)] * 2 + [sds((SEG1, D), BF16)] * 4,
        [half_slot] * 2 + [whole((SEG1, D))] * 4,
        scratch=[pltpu.VMEM((2 * ZW, D), F32)],
        prefetch=at, flops=6 * TOK * D * ZW,
    )
    dxi, dbi, dci, dcum, hall = call(
        inner_kernel, "inner", (GRP,), (xdt, bb, cc, info, rowc, dy, hloc, hin, grads1[0]),
        [rows(ZW), rows(ST), rows(ST), rows(LANES), rowspec, rows(ZW), hspec, whole((ZW, ST)), anyspec],
        [sds((TOK, ZW)), sds((TOK, ST)), sds((TOK, ST)), sds((TOK, LANES)), sds((GRP, ZW, ST))],
        [rows(ZW), rows(ST), rows(ST), rows(LANES), hspec], flops=2 * TOK * 8 * BLK * ZW,
    )
    hback = pl.BlockSpec((1, ZW, ST), lambda i, *_: (GRP - 1 - i, 0, 0))
    dpx, *dbc, draw, g_head = call(
        back_kernel, "back", (GRP,),
        (after, dxi, dbi, dci, dcum, hall, xa, px, bb, cc, info, dy, hp, skip),
        [whole((ZW, ST)), rows_back(ZW), rows_back(ST), rows_back(ST), rows_back(LANES), hback,
         rows_back(ZW), rows_back(ZW), rows_back(ST), rows_back(ST), rows_back(LANES),
         rows_back(ZW), whole((8, LANES)), whole((1, ZW))],
        [sds((TOK, ZW))] + [sds((TOK, 2 * SW), BF16)] * 4 + [sds((TOK, LANES), BF16), sds((8, LANES))],
        [rows_back(ZW)] + [rows_back(2 * SW)] * 4 + [rows_back(LANES), whole((8, LANES))],
        scratch=[pltpu.VMEM((ZW, ST), F32)], flops=2 * TOK * 4 * ST * ZW,
    )
    bc_got = [trade("head", b)(dbc[b]) for b in (1, 2, 3)]
    dpo, edge_back = call(
        edge_kernel, "edge", (GRP,), (dbc[0], *bc_got, po, dpx),
        [rows(2 * SW)] * 5 + [pl.BlockSpec((8, ZW), lambda i: (0, 0))],
        [sds((TOK, 2 * SW)), sds((8, ZW + LANES))], [rows(2 * SW), whole((8, ZW + LANES))],
    )
    halo_back = moved(edge_back, -GRP)
    keep_b, send_b, *grads2 = call(
        last_kernel, "last", (GRP,),
        (dpx, dpo, halo_back, mx, mo, conv_params, dz, draw, nrm, w, wdt, gain, g_gate, g_head),
        [rows_back(ZW), rows_back(2 * SW), whole((8, ZW + LANES)), rows_back(ZW), rows_back(2 * SW),
         whole((5, 1, 448)), rows_back(ZW),
         rows_back(LANES), rows_back(D), whole((WROWS, D)), whole((LANES, D)), whole((1, D)),
         whole((8, ZW)), whole((8, LANES))],
        [sds((GRP, HALF, D), BF16)] * 2 + [sds((SEG2, D), BF16)] * 4,
        [pl.BlockSpec((1, HALF, D), lambda i, at: ((GRP - 1 - i) ^ at[0], 0, 0))] * 2
        + [whole((SEG2, D))] * 4,
        scratch=[pltpu.VMEM((BLK + 8, ZW), F32), pltpu.VMEM((BLK + 8, 2 * SW), F32),
                 pltpu.VMEM((GRP * SEG2, D), F32), pltpu.VMEM((LANES, D), F32),
                 pltpu.VMEM((8, D), F32), pltpu.VMEM((8, ZW), F32), pltpu.VMEM((8, 2 * SW), F32)],
        prefetch=at, flops=4 * TOK * D * 960,
    )

    out_parts = returned(at, keep, send)
    block_out = home(home_out_kernel, "home_out", at, lengths, (block_in,), (None,), out_parts, BF16)
    grad_parts = returned(at, keep_b, send_b)
    input_grad = home(
        home_grad_kernel, "home_grad", at, lengths, (block_in, cotangent, gain),
        (None, None, (1, D)), grad_parts, F32,
    )

    root = math.sqrt(TOK * lax.axis_size("seq"))
    sums1 = summed_over_seq(grads1, SEG1)
    mat = whole((ZW, D))
    turned3 = [turned(p) for p in (in_proj, in_proj_momentum, in_proj_average)]
    turned_shape = [sds((COLS, 1, D))] * 3
    buffers = [pltpu.VMEM((COLS, D), F32)] * 6 + [pltpu.SemaphoreType.DMA((5, 6))]
    out_w, out_m, out_a, *in_half = call(
        functools.partial(update_a_kernel, rate=RATES[5] / root, rate_in=RATES[1] / root), "update_a", (1,),
        (*sums1, out_proj, out_proj_momentum, out_proj_average, *turned3),
        [whole((SEG1, D))] * 4 + [mat] * 3 + [anyspec] * 3, [sds((ZW, D))] * 3 + turned_shape,
        [mat] * 3 + [anyspec] * 3, scratch=[pltpu.VMEM((2 * ZW, D), F32)] + buffers, prefetch=at,
    )
    sums2 = summed_over_seq(grads2, SEG2)
    *in_new, small = call(
        functools.partial(update_b_kernel, rate=RATES[1] / root), "update_b", (1,),
        (*sums2, *turned3, *in_half), [whole((SEG2, D))] * 4 + [anyspec] * 6,
        turned_shape + [sds((24, D))], [anyspec] * 3 + [whole((24, D))],
        scratch=[pltpu.VMEM((GRP * SEG2, D), F32)] + buffers, prefetch=at, aliases={8: 0, 9: 1, 10: 2},
    )
    hd, gg, ng = HD_AT - TAP_AT, GG_AT - TAP_AT, NG_AT - TAP_AT
    g_taps = small[0:5, 0:448].reshape(5, 1, 448)
    g_heads = small[hd : hd + 3, 0:NH]
    g_ggain = small[gg, 0:ZW]
    own_norm = small[ng]
    g_norm = own_norm
    for b in (1, 2, 3):
        g_norm = g_norm + trade("head", b)(own_norm)
    ng3 = advance(norm_gain, g_norm, norm_gain_momentum, norm_gain_average, RATES[0] / root)
    cv3 = advance(conv_params, g_taps, conv_momentum, conv_average, RATES[2] / root)
    hd3 = advance(head_params, g_heads, head_momentum, head_average, RATES[3] / root)
    gg3 = advance(gate_gain, g_ggain, gate_gain_momentum, gate_gain_average, RATES[4] / root)
    in3 = tuple(turned(a) for a in in_new)
    return (block_out, input_grad, *ng3, *in3, *cv3, *hd3, *gg3, out_w, out_m, out_a)


def solution(mesh):
    act, vec, mat = P(None, "seq", None), P(), P(None, "head", None)
    weights = (vec, mat, mat, P(None, "head"), P("head"), P("head", None))
    outs = tuple(spec for spec in weights for _ in range(3))
    return jax.shard_map(
        shards,
        mesh=mesh,
        in_specs=(act, act, P(), *weights, *weights, *weights),
        out_specs=(act, act, *outs),
        check_vma=False,
    )
```

time: 618 us -> 247 us (0.40); the launches traced: 609 us -> 247 us
  waiting for transfers between devices: 263 us -> 77 us
  other arithmetic: 121 us -> 3.07 us
  Pallas kernels: 0 us -> 90.9 us
  blocking collectives: 85.5 us -> 0 us
  matrix products: 66.2 us -> 0 us
  starting transfers between devices: 7.05 us -> 58.7 us
  local copies, waits for them, and re-layouts: 49.1 us -> 15.3 us
  between operations: 16 us -> 1.7 us
    psum x2 -> x0, waiting for transfers between devices: 210 us -> none  [the longest x1 109 us: shards(): branch = lax.psum(partial_out, 'head').reshape(seq_count, blk_rows, width)]
    pallas_call x0 -> x25, Pallas kernels: none -> 90.9 us  [the longest x23 80 us: call(): pl.pallas_call(kernel, grid_spec=spec, out_shape=outs, compiler_params=pa...]
    ppermute x2 -> x54, waiting for transfers between devices: 0.01 us -> 77 us  [the longest x50 75.3 us: trade(): return lambda array: lax.ppermute(array, axis, pairs)]
    dot_general x18 -> x0, matrix products: 66.2 us -> none  [the longest x3 27.7 us: span_parts(): jnp.einsum('tsh,shp->thp', weights, step_sizes[:, :, None] * x_values, pr...]
    all_gather x2 -> x0, waiting for transfers between devices: 53.6 us -> none  [the longest x1 28 us: prefix_2(): lax.all_gather(part.astype(kind), axis)]
    ppermute x2 -> x54, starting transfers between devices: 6.38 us -> 58.7 us  [the longest x50 50 us: trade(): return lambda array: lax.ppermute(array, axis, pairs)]
    psum x3 -> x0, blocking collectives: 51.7 us -> none  [the longest x1 39.4 us: shards(): lax.psum((g_ngain, g_in, g_taps, g_heads, g_ggain, g_out), 'seq')]
    another operation x7 -> x4, other arithmetic: 40.2 us -> 1.18 us  [the longest x1 0.98 us: shards(): cot_own = jnp.stack(cot_got)]
  transfers between devices with their start and end apart: 7 -> 54, of which waited for: 4 -> 20; matrix products, arithmetic and copies ran while one was open for 21% -> 3% of each run, Pallas kernels for 0% -> 26%
where the time goes in v1:
time: 247 us
  Pallas kernels  90.9 us (37%)
  waiting for transfers between devices  77 us (31%)
  starting transfers between devices  58.7 us (24%)
  local copies, waits for them, and re-layouts  15.3 us (6%)
  other arithmetic  3.07 us (1%)
    pallas_call x23, Pallas kernels, call(): pl.pallas_call(kernel, grid_spec=spec, out_shape=outs, compiler_params=pa...  80 us
    ppermute x50, waiting for transfers between devices, trade(): return lambda array: lax.ppermute(array, axis, pairs)  75.3 us
    ppermute x50, starting transfers between devices, trade(): return lambda array: lax.ppermute(array, axis, pairs)  50 us
    unnamed x125, local copies, waits for them, and re-layouts  11 us
    pallas_call x2, Pallas kernels, home(): pl.pallas_call(kernel, grid_spec=spec, out_shape=sds((GRP, BLK, D), dtype...  10.8 us
    ppermute x4, starting transfers between devices, moved(): return lax.ppermute(array, 'seq', pairs)  8.65 us
  transfers between devices with their start and end apart: 54, of which 20 were waited for; matrix products, arithmetic and copies ran while one was open for 3% of the time, Pallas kernels for 26%

profile of v1, /device:TPU:0, one launch (start us, length us, event | category | flops | bytes accessed | tf_op | source)
XLA Modules:
  0.0 246.6 jit_solution(10025967969049838795)
XLA Ops:
  9.3 3.3 %collective-permute-done = bf16[128,768]{1,0:T(8,128)(2,1)S(1)} collective-permute-done((bf16[128,768]{1,0:T(8,128)(2,1)S(1)}, bf16[128,768]{1,0:T(8,128)(2,1)S(1)}, u32[]{:S(2)}, u32[]{:S(2)}) %collective-permute-start) | collective-permute-done | bytes 196640 | tf_op jit(solution)/shard_map/ppermute | solution.py:701
  22.4 3.4 %collective-permute-done.8 = bf16[128,768]{1,0:T(8,128)(2,1)S(1)} collective-permute-done((bf16[128,768]{1,0:T(8,128)(2,1)S(1)}, bf16[128,768]{1,0:T(8,128)(2,1)S(1)}, u32[]{:S(2)}, u32[]{:S(2)}) %collective-permute-start.8) | collective-permute-done | bytes 196640 | tf_op jit(solution)/shard_map/ppermute | solution.py:701
  39.1 4.5 %collective-permute-start.4 = (bf16[16,768]{1,0:T(8,128)(2,1)S(1)}, bf16[16,768]{1,0:T(8,128)(2,1)S(1)}, u32[]{:S(2)}, u32[]{:S(2)}) collective-permute-start(bf16[16,768]{1,0:T(8,128)(2,1)S(1)} %fusion), channel_id=1, source_target_pairs={{0,16},{4,20},{8,24},{12,28},{1,17},{5,21},{9,25},{13,29},{2,18},{... | collective-permute-start | bytes 73736 | tf_op jit(solution)/shard_map/ppermute | solution.py:707
  43.6 7.7 %first.1 = (bf16[1024,768]{1,0:T(8,128)(2,1)S(1)}, f32[1024,384]{1,0:T(8,128)S(1)}, f32[1024,128]{1,0:T(8,128)S(1)}, f32[8,1024]{1,0:T(8,128)S(1)}, f32[8,128]{1,0:T(8,128)}) custom-call(s32[5]{0:T(128)S(1)} %stack.79.at, bf16[4,128,768]{2,1,0:T(8,128)(2,1)S(1)} %pad_maximum_fusion.own.refs_4_, bf16[4,128,768]{2,1,0:T(8,128)(2,1)} %collective-permute-done.3.oth, ...), custom_call_target="tpu_custom_call" | custom-call | flops 805306368 | bytes 6761472 | tf_op jit(solution)/shard_map/first/pallas_call | solution.py:100
  52.1 8.4 %mix.1 = (f32[1024,384]{1,0:T(8,128)S(1)}, f32[1024,384]{1,0:T(8,128)S(1)}, f32[1024,384]{1,0:T(8,128)S(1)}, bf16[1024,384]{1,0:T(8,128)(2,1)S(1)}, f32[1024,64]...) custom-call(bf16[1024,768]{1,0:T(8,128)(2,1)S(1)} %get-tuple-element, ...), custom_call_target="tpu_custom_call" | custom-call | flops 1107296256 | bytes 12619520 | tf_op jit(solution)/shard_map/mix/pallas_call | solution.py:100
  63.4 6.0 %local.1 = (f32[1024,384]{1,0:T(8,128)S(1)}, f32[1024,384]{1,0:T(8,128)S(1)}, bf16[1024,768]{1,0:T(8,128)(2,1)S(1)}) custom-call(s32[5]{0:T(128)S(1)} %stack.79.at, bf16[1024,384]{1,0:T(8,128)(2,1)S(1)} %get-tuple-element.113.xdt, f32[1024,384]{1,0:T(8,128)S(1)} %get-tuple-element.114.xa, bf16[1024,128]{1,0:T(8,128)(2,1)S(1)} %get-tuple-element.115.b, ...), custom_call_target="tpu_custom_call" | custom-call | flops 1409286144 | bytes 11109888 | tf_op jit(solution)/shard_map/local/pallas_call | solution.py:100
  77.7 3.8 %ungate.1 = (f32[1024,384]{1,0:T(8,128)S(1)}, bf16[1024,384]{1,0:T(8,128)(2,1)S(1)}, bf16[1024,384]{1,0:T(8,128)(2,1)S(1)}, bf16[384,128]{1,0:T(8,128)(2,1)S(1)}, f32[8,384]{1,0:T(8,128)S(1)}) custom-call(f32[1024,384]{1,0:T(8,128)S(1)} %get-tuple-element.128.y, f32[1024,384]{1,0:T(8,128)S(1)} %get-tuple-element.126.z, ...), custom_call_target="tpu_custom_call" | custom-call | flops 100663296 | bytes 8893952 | tf_op jit(solution)/shard_map/ungate/pallas_call | solution.py:100
  83.1 4.7 %out.1 = (bf16[4,128,768]{2,1,0:T(8,128)(2,1)S(1)}, bf16[4,128,768]{2,1,0:T(8,128)(2,1)}, bf16[192,768]{1,0:T(8,128)(2,1)S(1)}, bf16[192,768]{1,0:T(8,128)(2,1)}...) custom-call(s32[5]{0:T(128)S(1)} %stack.79.at, bf16[1024,384]{1,0:T(8,128)(2,1)S(1)} %get-tuple-element.130.yn, ...), custom_call_target="tpu_custom_call" | custom-call | flops 1811939328 | bytes 8060928 | tf_op jit(solution)/shard_map/out/pallas_call | solution.py:100
  87.8 8.2 %inner.1 = (f32[1024,384]{1,0:T(8,128)S(1)}, f32[1024,128]{1,0:T(8,128)S(1)}, f32[1024,128]{1,0:T(8,128)S(1)}, f32[1024,128]{1,0:T(8,128)S(1)}, f32[4,384,128]{2,1,0:T(8,128)S(1)}) custom-call(bf16[1024,384]{1,0:T(8,128)(2,1)S(1)} %copy-done.12, bf16[1024,128]{1,0:T(8,128)(2,1)S(1)} %get-tuple-element.115.b, bf16[1024,128]{1,0:T(8,128)(2,1)S(1)} %get-tuple-element.116.c, ...), custom_call_target="tpu_custom_call" | custom-call | flops 1610612736 | bytes 8552448 | tf_op jit(solution)/shard_map/inner/pallas_call | solution.py:100
  96.1 12.0 %back.1 = (f32[1024,384]{1,0:T(8,128)S(1)}, bf16[1024,64]{1,0:T(8,128)(2,1)S(1)}, bf16[1024,64]{1,0:T(8,128)(2,1)S(1)}, bf16[1024,64]{1,0:T(8,128)(2,1)S(1)}, bf...) custom-call(bf16[384,128]{1,0:T(8,128)(2,1)S(1)} %collective-permute-done.24.after, ...), custom_call_target="tpu_custom_call" | custom-call | flops 402653184 | bytes 12166656 | tf_op jit(solution)/shard_map/back/pallas_call | solution.py:100
  110.0 7.3 %collective-permute-done.26.r2 = bf16[1024,64]{1,0:T(8,128)(2,1)S(1)} collective-permute-done((bf16[1024,64]{1,0:T(8,128)(2,1)S(1)}, bf16[1024,64]{1,0:T(8,128)(2,1)S(1)}, u32[]{:S(2)}, u32[]{:S(2)}) %collective-permute-start.26) | collective-permute-done | bytes 131104 | tf_op jit(solution)/shard_map/ppermute | solution.py:701
  117.3 4.7 %collective-permute-done.27.r3 = bf16[1024,64]{1,0:T(8,128)(2,1)S(1)} collective-permute-done((bf16[1024,64]{1,0:T(8,128)(2,1)S(1)}, bf16[1024,64]{1,0:T(8,128)(2,1)S(1)}, u32[]{:S(2)}, u32[]{:S(2)}) %collective-permute-start.27) | collective-permute-done | bytes 131104 | tf_op jit(solution)/shard_map/ppermute | solution.py:701
  130.5 6.4 %last.1 = (bf16[4,128,768]{2,1,0:T(8,128)(2,1)S(1)}, bf16[4,128,768]{2,1,0:T(8,128)(2,1)S(1)}, bf16[120,768]{1,0:T(8,128)(2,1)S(1)}, bf16[120,768]{1,0:T(8,128)(...) custom-call(s32[5]{0:T(128)S(1)} %stack.79.at, f32[1024,384]{1,0:T(8,128)S(1)} %get-tuple-element.150.dpx, ...), custom_call_target="tpu_custom_call" | custom-call | flops 3019898880 | bytes 10120960 | tf_op jit(solution)/shard_map/last/pallas_call | solution.py:100
  137.1 4.1 %collective-permute-done.46.refs_3_ = bf16[192,768]{1,0:T(8,128)(2,1)S(1)} collective-permute-done((bf16[192,768]{1,0:T(8,128)(2,1)}, bf16[192,768]{1,0:T(8,128)(2,1)S(1)}, u32[]{:S(2)}, u32[]{:S(2)}) %collective-permute-start.46) | collective-permute-done | bytes 294944 | tf_op jit(solution)/shard_map/ppermute | solution.py:701
  147.5 9.7 %collective-permute-done.47.refs_1_ = bf16[192,768]{1,0:T(8,128)(2,1)S(1)} collective-permute-done((bf16[192,768]{1,0:T(8,128)(2,1)S(1)}, bf16[192,768]{1,0:T(8,128)(2,1)S(1)}, u32[]{:S(2)}, u32[]{:S(2)}) %collective-permute-start.47) | collective-permute-done | bytes 294944 | tf_op jit(solution)/shard_map/ppermute | solution.py:701
  160.9 4.6 %collective-permute-done.39.refs_3_ = bf16[120,768]{1,0:T(8,128)(2,1)S(1)} collective-permute-done((bf16[120,768]{1,0:T(8,128)(2,1)S(1)}, bf16[120,768]{1,0:T(8,128)(2,1)S(1)}, u32[]{:S(2)}, u32[]{:S(2)}) %collective-permute-start.39) | collective-permute-done | bytes 184352 | tf_op jit(solution)/shard_map/ppermute | solution.py:701
  170.9 8.5 %collective-permute-done.40.refs_1_ = bf16[120,768]{1,0:T(8,128)(2,1)S(1)} collective-permute-done((bf16[120,768]{1,0:T(8,128)(2,1)S(1)}, bf16[120,768]{1,0:T(8,128)(2,1)S(1)}, u32[]{:S(2)}, u32[]{:S(2)}) %collective-permute-start.40) | collective-permute-done | bytes 184352 | tf_op jit(solution)/shard_map/ppermute | solution.py:701
  180.1 4.2 %collective-permute-start.43 = (bf16[120,768]{1,0:T(8,128)(2,1)S(1)}, bf16[120,768]{1,0:T(8,128)(2,1)S(1)}, u32[]{:S(2)}, u32[]{:S(2)}) collective-permute-start(bf16[120,768]{1,0:T(8,128)(2,1)S(1)} %sum.5.g0), channel_id=1, source_target_pairs={{0,12},{4,8},{8,4},{12,0},{16,28},{20,24},{24,20},{28,16},{1,13},{... | collective-permute-start | bytes 552968 | tf_op jit(solution)/shard_map/ppermute | solution.py:701
  185.0 7.4 %update_a.1 = (f32[384,768]{1,0:T(8,128)}, f32[384,768]{1,0:T(8,128)}, f32[384,768]{1,0:T(8,128)}, f32[838,1,768]{2,1,0:T(1,128)}, f32[838,1,768]{2,1,0:T(1,128)}, /*index=5*/f32[838,1,768]{2,1,0:T(1,128)}) custom-call(s32[5]{0:T(128)S(1)} %stack.79.at, bf16[192,768]{1,0:T(8,128)(2,1)S(1)} %sum.7.g0, bf16[192,768]{1,0:T(8,128)(2,1)S(1)} %collective-permute-done.48.g1, ...), custom_call_target="tpu_custom_call" | custom-call | bytes 23703552 | tf_op jit(solution)/shard_map/update_a/pallas_call | solution.py:100
  192.4 5.8 %update_b.1 = (f32[838,1,768]{2,1,0:T(1,128)}, f32[838,1,768]{2,1,0:T(1,128)}, f32[838,1,768]{2,1,0:T(1,128)}, f32[24,768]{1,0:T(8,128)S(1)}) custom-call(s32[5]{0:T(128)S(1)} %stack.79.at, bf16[120,768]{1,0:T(8,128)(2,1)S(1)} %sum.5.g0, ...), custom_call_target="tpu_custom_call", output_to_operand_aliasing={{0}: (8, {}), {1}: (9, {}), {2}: (10, {})} | custom-call | bytes 23980032 | tf_op jit(solution)/shard_map/update_b/pallas_call | solution.py:100
  215.8 7.2 %collective-permute-done.21.x = bf16[4,64,768]{2,1,0:T(8,128)(2,1)S(1)} collective-permute-done((bf16[4,64,768]{2,1,0:T(8,128)(2,1)S(1)}, bf16[4,64,768]{2,1,0:T(8,128)(2,1)S(1)}, u32[]{:S(2)}, u32[]{:S(2)}) %collective-permute-start.21) | collective-permute-done | bytes 393248 | tf_op jit(solution)/shard_map/ppermute | solution.py:701
  223.0 6.5 %collective-permute-done.34.x = bf16[4,64,768]{2,1,0:T(8,128)(2,1)S(1)} collective-permute-done((bf16[4,64,768]{2,1,0:T(8,128)(2,1)S(1)}, bf16[4,64,768]{2,1,0:T(8,128)(2,1)S(1)}, u32[]{:S(2)}, u32[]{:S(2)}) %collective-permute-start.34) | collective-permute-done | bytes 393248 | tf_op jit(solution)/shard_map/ppermute | solution.py:701
  234.2 4.9 %home_out.1 = bf16[4,256,768]{2,1,0:T(8,128)(2,1)} custom-call(s32[5]{0:T(128)} %copy-done.23, s32[4]{0:T(128)} %lens.3, bf16[4,256,768]{2,1,0:T(8,128)(2,1)} %block.3, bf16[4,64,768]{2,1,0:T(8,128)(2,1)} %copy-done.40, bf16[4,64,768]{2,1,0:T(8,128)(2,1)} %copy-done.44, bf16[4,64,768]{2,1,0:T(8,128)(2,1)} %copy-done.45, bf16[4,64,768]{2,1,0:T(8,128)(2,1)} %copy-done.46), custom_call_target="tpu_custom_call" | custom-call | bytes 8388608 | tf_op jit(solution)/shard_map/home_out/pallas_call | solution.py:613
  240.7 5.9 %home_grad.1 = f32[4,256,768]{2,1,0:T(8,128)} custom-call(s32[5]{0:T(128)} %copy-done.23, s32[4]{0:T(128)} %lens.3, bf16[4,256,768]{2,1,0:T(8,128)(2,1)} %block.3, bf16[4,256,768]{2,1,0:T(8,128)(2,1)} %cot.1, f32[1,768]{1,0:T(1,128)} %copy-done.24, bf16[4,64,768]{2,1,0:T(8,128)(2,1)} %copy-done.39, bf16[4,64,768]{2,1,0:T(8,128)(2,1)} %copy-done.41, ...), custom_call_target="tpu_custom_call" | custom-call | bytes 8388608 | tf_op jit(solution)/shard_map/home_grad/pallas_call | solution.py:613
  (257 shorter events, 95.7 us)
Async XLA Ops:
  22.4 15.8 %collective-permute-start.3 = (bf16[4,128,768]{2,1,0:T(8,128)(2,1)S(1)}, bf16[4,128,768]{2,1,0:T(8,128)(2,1)}, u32[]{:S(2)}, u32[]{:S(2)}) collective-permute-start(bf16[4,128,768]{2,1,0:T(8,128)(2,1)S(1)} %pad_maximum_fusion.own.refs_4_), channel_id=1, source_target_pairs={{0,1},{1,0},{2,3},{3,2},{4,5},{5,4},{6,7},{7,6},{8,9},{9,8},{10,11... | collective-permute-start | bytes 2359304 | tf_op jit(solution)/shard_map/ppermute | solution.py:701
  31.1 32.3 %collective-permute-start.11 = (bf16[4,128,768]{2,1,0:T(8,128)(2,1)}, bf16[4,128,768]{2,1,0:T(8,128)(2,1)}, u32[]{:S(2)}, u32[]{:S(2)}) collective-permute-start(bf16[4,128,768]{2,1,0:T(8,128)(2,1)} %pad_maximum_fusion.1.own), channel_id=1, source_target_pairs={{0,1},{1,0},{2,3},{3,2},{4,5},{5,4},{6,7},{7,6},{8,9},{9,8},{10,11... | collective-permute-start | bytes 2359304 | tf_op jit(solution)/shard_map/ppermute | solution.py:701
  34.6 16.7 %collective-permute-start.7 = (bf16[80,768]{1,0:T(8,128)(2,1)}, bf16[80,768]{1,0:T(8,128)(2,1)}, u32[]{:S(2)}, u32[]{:S(2)}) collective-permute-start(bf16[80,768]{1,0:T(8,128)(2,1)} %get-tuple-element.111.bc0), channel_id=1, source_target_pairs={{0,3},{1,2},{2,1},{3,0},{4,7},{5,6},{6,5},{7,4},{8,11},{9,10},{10,... | collective-permute-start | bytes 368648 | tf_op jit(solution)/shard_map/ppermute | solution.py:701
  36.2 15.2 %collective-permute-start.6 = (bf16[80,768]{1,0:T(8,128)(2,1)}, bf16[80,768]{1,0:T(8,128)(2,1)}, u32[]{:S(2)}, u32[]{:S(2)}) collective-permute-start(bf16[80,768]{1,0:T(8,128)(2,1)} %get-tuple-element.111.bc0), channel_id=1, source_target_pairs={{0,2},{1,3},{2,0},{3,1},{4,6},{5,7},{6,4},{7,5},{8,10},{9,11},{10,... | collective-permute-start | bytes 368648 | tf_op jit(solution)/shard_map/ppermute | solution.py:701
  36.8 14.6 %collective-permute-start.5 = (bf16[80,768]{1,0:T(8,128)(2,1)}, bf16[80,768]{1,0:T(8,128)(2,1)}, u32[]{:S(2)}, u32[]{:S(2)}) collective-permute-start(bf16[80,768]{1,0:T(8,128)(2,1)} %get-tuple-element.111.bc0), channel_id=1, source_target_pairs={{0,1},{1,0},{2,3},{3,2},{4,5},{5,4},{6,7},{7,6},{8,9},{9,8},{10,11... | collective-permute-start | bytes 368648 | tf_op jit(solution)/shard_map/ppermute | solution.py:701
  81.5 14.5 %collective-permute-start.24 = (bf16[384,128]{1,0:T(8,128)(2,1)S(1)}, bf16[384,128]{1,0:T(8,128)(2,1)S(1)}, u32[]{:S(2)}, u32[]{:S(2)}) collective-permute-start(bf16[384,128]{1,0:T(8,128)(2,1)S(1)} %get-tuple-element.141), channel_id=1, source_target_pairs={{16,0},{20,4},{24,8},{28,12},{17,1},{21,5},{25,9},{29,13},{18,2},{... | collective-permute-start | bytes 294920 | tf_op jit(solution)/shard_map/ppermute | solution.py:707
  108.8 13.2 %collective-permute-start.27 = (bf16[1024,64]{1,0:T(8,128)(2,1)S(1)}, bf16[1024,64]{1,0:T(8,128)(2,1)S(1)}, u32[]{:S(2)}, u32[]{:S(2)}) collective-permute-start(bf16[1024,64]{1,0:T(8,128)(2,1)S(1)} %get-tuple-element.154), channel_id=1, source_target_pairs={{0,3},{1,2},{2,1},{3,0},{4,7},{5,6},{6,5},{7,4},{8,11},{9,10},{10,... | collective-permute-start | bytes 393224 | tf_op jit(solution)/shard_map/ppermute | solution.py:701
  123.8 13.2 %collective-permute-start.44 = (bf16[192,768]{1,0:T(8,128)(2,1)}, bf16[192,768]{1,0:T(8,128)(2,1)S(1)}, u32[]{:S(2)}, u32[]{:S(2)}) collective-permute-start(bf16[192,768]{1,0:T(8,128)(2,1)} %get-tuple-element.175), channel_id=1, source_target_pairs={{0,4},{4,0},{8,12},{12,8},{16,20},{20,16},{24,28},{28,24},{1,5},{5... | collective-permute-start | bytes 884744 | tf_op jit(solution)/shard_map/ppermute | solution.py:701
  126.8 14.3 %collective-permute-start.46 = (bf16[192,768]{1,0:T(8,128)(2,1)}, bf16[192,768]{1,0:T(8,128)(2,1)S(1)}, u32[]{:S(2)}, u32[]{:S(2)}) collective-permute-start(bf16[192,768]{1,0:T(8,128)(2,1)} %get-tuple-element.177), channel_id=1, source_target_pairs={{0,12},{4,8},{8,4},{12,0},{16,28},{20,24},{24,20},{28,16},{1,13},{... | collective-permute-start | bytes 884744 | tf_op jit(solution)/shard_map/ppermute | solution.py:701
  127.4 39.8 %collective-permute-start.16 = (bf16[4,128,768]{2,1,0:T(8,128)(2,1)}, bf16[4,128,768]{2,1,0:T(8,128)(2,1)S(1)}, u32[]{:S(2)}, u32[]{:S(2)}) collective-permute-start(bf16[4,128,768]{2,1,0:T(8,128)(2,1)} %get-tuple-element.134), channel_id=1, source_target_pairs={{0,1},{1,0},{2,3},{3,2},{4,5},{5,4},{6,7},{7,6},{8,9},{9,8},{10,11... | collective-permute-start | bytes 2359304 | tf_op jit(solution)/shard_map/ppermute | solution.py:701
  137.0 32.2 %collective-permute-start.29 = (bf16[4,128,768]{2,1,0:T(8,128)(2,1)S(1)}, bf16[4,128,768]{2,1,0:T(8,128)(2,1)S(1)}, u32[]{:S(2)}, u32[]{:S(2)}) collective-permute-start(bf16[4,128,768]{2,1,0:T(8,128)(2,1)S(1)} %get-tuple-element.164), channel_id=1, source_target_pairs={{0,1},{1,0},{2,3},{3,2},{4,5},{5,4},{6,7},{7,6},{8,9},{9,8},{10,11... | collective-permute-start | bytes 2359304 | tf_op jit(solution)/shard_map/ppermute | solution.py:701
  141.3 15.9 %collective-permute-start.47 = (bf16[192,768]{1,0:T(8,128)(2,1)S(1)}, bf16[192,768]{1,0:T(8,128)(2,1)S(1)}, u32[]{:S(2)}, u32[]{:S(2)}) collective-permute-start(bf16[192,768]{1,0:T(8,128)(2,1)S(1)} %sum.6.refs_0_), channel_id=1, source_target_pairs={{0,16},{4,20},{8,24},{12,28},{16,0},{20,4},{24,8},{28,12},{1,17},{... | collective-permute-start | bytes 884744 | tf_op jit(solution)/shard_map/ppermute | solution.py:701
  144.5 14.2 %collective-permute-start.37 = (bf16[120,768]{1,0:T(8,128)(2,1)S(1)}, bf16[120,768]{1,0:T(8,128)(2,1)S(1)}, u32[]{:S(2)}, u32[]{:S(2)}) collective-permute-start(bf16[120,768]{1,0:T(8,128)(2,1)S(1)} %get-tuple-element.172), channel_id=1, source_target_pairs={{0,4},{4,0},{8,12},{12,8},{16,20},{20,16},{24,28},{28,24},{1,5},{5... | collective-permute-start | bytes 552968 | tf_op jit(solution)/shard_map/ppermute | solution.py:701
  145.9 14.3 %collective-permute-start.38 = (bf16[120,768]{1,0:T(8,128)(2,1)S(1)}, bf16[120,768]{1,0:T(8,128)(2,1)S(1)}, u32[]{:S(2)}, u32[]{:S(2)}) collective-permute-start(bf16[120,768]{1,0:T(8,128)(2,1)S(1)} %get-tuple-element.173), channel_id=1, source_target_pairs={{0,8},{4,12},{8,0},{12,4},{16,24},{20,28},{24,16},{28,20},{1,9},{5... | collective-permute-start | bytes 552968 | tf_op jit(solution)/shard_map/ppermute | solution.py:701
  158.8 21.3 %collective-permute-start.50 = (bf16[192,768]{1,0:T(8,128)(2,1)S(1)}, bf16[192,768]{1,0:T(8,128)(2,1)S(1)}, u32[]{:S(2)}, u32[]{:S(2)}) collective-permute-start(bf16[192,768]{1,0:T(8,128)(2,1)S(1)} %sum.7.g0), channel_id=1, source_target_pairs={{0,12},{4,8},{8,4},{12,0},{16,28},{20,24},{24,20},{28,16},{1,13},{... | collective-permute-start | bytes 884744 | tf_op jit(solution)/shard_map/ppermute | solution.py:701
  160.2 24.1 %collective-permute-start.49 = (bf16[192,768]{1,0:T(8,128)(2,1)S(1)}, bf16[192,768]{1,0:T(8,128)(2,1)S(1)}, u32[]{:S(2)}, u32[]{:S(2)}) collective-permute-start(bf16[192,768]{1,0:T(8,128)(2,1)S(1)} %sum.7.g0), channel_id=1, source_target_pairs={{0,8},{4,12},{8,0},{12,4},{16,24},{20,28},{24,16},{28,20},{1,9},{5... | collective-permute-start | bytes 884744 | tf_op jit(solution)/shard_map/ppermute | solution.py:701
  165.5 18.8 %collective-permute-start.48 = (bf16[192,768]{1,0:T(8,128)(2,1)S(1)}, bf16[192,768]{1,0:T(8,128)(2,1)S(1)}, u32[]{:S(2)}, u32[]{:S(2)}) collective-permute-start(bf16[192,768]{1,0:T(8,128)(2,1)S(1)} %sum.7.g0), channel_id=1, source_target_pairs={{0,4},{4,0},{8,12},{12,8},{16,20},{20,16},{24,28},{28,24},{1,5},{5... | collective-permute-start | bytes 884744 | tf_op jit(solution)/shard_map/ppermute | solution.py:701
  169.2 29.1 %collective-permute-start.17 = (bf16[4,64,768]{2,1,0:T(8,128)(2,1)S(1)}, bf16[4,64,768]{2,1,0:T(8,128)(2,1)S(1)}, u32[]{:S(2)}, u32[]{:S(2)}) collective-permute-start(bf16[4,64,768]{2,1,0:T(8,128)(2,1)S(1)} %get-tuple-element.136), channel_id=1, source_target_pairs={{0,2},{1,3},{2,0},{3,1},{4,6},{5,7},{6,4},{7,5},{8,10},{9,11},{10,... | collective-permute-start | bytes 1179656 | tf_op jit(solution)/shard_map/ppermute | solution.py:701
  179.4 22.8 %collective-permute-start.30 = (bf16[4,64,768]{2,1,0:T(8,128)(2,1)S(1)}, bf16[4,64,768]{2,1,0:T(8,128)(2,1)S(1)}, u32[]{:S(2)}, u32[]{:S(2)}) collective-permute-start(bf16[4,64,768]{2,1,0:T(8,128)(2,1)S(1)} %get-tuple-element.166), channel_id=1, source_target_pairs={{0,2},{1,3},{2,0},{3,1},{4,6},{5,7},{6,4},{7,5},{8,10},{9,11},{10,... | collective-permute-start | bytes 1179656 | tf_op jit(solution)/shard_map/ppermute | solution.py:701
  202.1 13.2 %collective-permute-start.53 = (f32[768]{0:T(1024)S(1)}, f32[768]{0:T(1024)S(1)}, u32[]{:S(2)}, u32[]{:S(2)}) collective-permute-start(f32[768]{0:T(1024)S(1)} %slice_reduce_fusion), channel_id=1, source_target_pairs={{0,3},{1,2},{2,1},{3,0},{4,7},{5,6},{6,5},{7,4},{8,11},{9,10},{10,... | collective-permute-start | bytes 9224 | tf_op jit(solution)/shard_map/ppermute | solution.py:701
  209.6 22.5 %collective-permute-start.51 = (f32[768]{0:T(1024)S(1)}, f32[768]{0:T(1024)S(1)}, u32[]{:S(2)}, u32[]{:S(2)}) collective-permute-start(f32[768]{0:T(1024)S(1)} %slice_reduce_fusion), channel_id=1, source_target_pairs={{0,1},{1,0},{2,3},{3,2},{4,5},{5,4},{6,7},{7,6},{8,9},{9,8},{10,11... | collective-permute-start | bytes 9224 | tf_op jit(solution)/shard_map/ppermute | solution.py:701
  213.2 16.3 %collective-permute-start.34 = (bf16[4,64,768]{2,1,0:T(8,128)(2,1)S(1)}, bf16[4,64,768]{2,1,0:T(8,128)(2,1)S(1)}, u32[]{:S(2)}, u32[]{:S(2)}) collective-permute-start(bf16[4,64,768]{2,1,0:T(8,128)(2,1)S(1)} %pad_maximum_fusion.3.a), channel_id=1, source_target_pairs={{0,2},{1,3},{2,0},{3,1},{4,6},{5,7},{6,4},{7,5},{8,10},{9,11},{10,... | collective-permute-start | bytes 1179656 | tf_op jit(solution)/shard_map/ppermute | solution.py:701
  215.3 17.4 %collective-permute-start.22 = (bf16[4,64,768]{2,1,0:T(8,128)(2,1)S(1)}, bf16[4,64,768]{2,1,0:T(8,128)(2,1)S(1)}, u32[]{:S(2)}, u32[]{:S(2)}) collective-permute-start(bf16[4,64,768]{2,1,0:T(8,128)(2,1)S(1)} %pad_maximum_fusion.2.a), channel_id=1, source_target_pairs={{0,1},{1,0},{2,3},{3,2},{4,5},{5,4},{6,7},{7,6},{8,9},{9,8},{10,11... | collective-permute-start | bytes 1179656 | tf_op jit(solution)/shard_map/ppermute | solution.py:701
  215.3 23.8 %collective-permute-start.35 = (bf16[4,64,768]{2,1,0:T(8,128)(2,1)S(1)}, bf16[4,64,768]{2,1,0:T(8,128)(2,1)S(1)}, u32[]{:S(2)}, u32[]{:S(2)}) collective-permute-start(bf16[4,64,768]{2,1,0:T(8,128)(2,1)S(1)} %pad_maximum_fusion.3.a), channel_id=1, source_target_pairs={{0,1},{1,0},{2,3},{3,2},{4,5},{5,4},{6,7},{7,6},{8,9},{9,8},{10,11... | collective-permute-start | bytes 1179656 | tf_op jit(solution)/shard_map/ppermute | solution.py:701
  (91 other events, 1265.6 us)
